TPU v7x, 128 devices: a whole 4x4x4 slice. The times are simulated.
128 devices in a mesh: row: 8 (over x_hi, z), col: 16 (over y, x_lo, core).
Axes of the slice: x: 4 (x_hi: 2, x_lo: 2; x = x_hi * 2 + x_lo), y: 4, z: 4, core: 2. Of those that a mesh axis runs over, the one named last changes fastest.
Arguments:
- voxels: bfloat16 [32, 128, 256, 256], P(None, 'row', 'col'), may hold values from -6 to 6
- target: bfloat16 [32, 128, 256, 256], P(None, 'row', 'col'), may hold values from -6 to 6
- weight: bfloat16 [2, 32, 32, 64, 64, 32], P(None, None, None, 'row', 'col'), may hold values from -0.75 to 0.75
Outputs:
- grad_voxels: bfloat16 [32, 128, 256, 256], P(None, 'row', 'col')
- grad_weight: bfloat16 [2, 32, 32, 64, 64, 32], P(None, None, None, 'row', 'col')
All inputs are finite; a program needn't handle non-finite values.
Results may differ from a plain program's by a relative error of at most 0.0011.
Values sent between devices are 32-bit elements; how exact they have to be, the bound alone decides.
No kernel may reach another device: no remote copies, remote signals or barrier semaphores. Data moves between devices by JAX's collectives and lax.ppermute only.
A program may use at most 192 MiB of HBM per device.

v0:
```python
import functools
import math

import jax
import jax.numpy as jnp
import ml_dtypes
import numpy as np
from jax import lax
from jax.experimental import pallas as pl
from jax.experimental.pallas import tpu as pltpu
from jax.sharding import Mesh
from jax.sharding import PartitionSpec as P

C = 32
X = 128
Y = 256
Z = 256
MX = 32
MY = 64
MZ = 64

AXES = ("xh", "z", "y", "xl", "core")
SHAPE = (2, 4, 4, 2, 2)
ROW = ("xh", "z")
COL = ("y", "xl", "core")
FIRST = ("y", "core")
SECOND = ("xh", "z", "xl")
F32 = jnp.float32
BF16 = jnp.bfloat16


def split_parts(table):
    high = table.astype(ml_dtypes.bfloat16)
    low = (table - high.astype(np.float64)).astype(ml_dtypes.bfloat16)
    return high, low


def angles(frequency, position, length):
    return 2.0 * np.pi / length * ((frequency[:, None] * position[None, :]) % length)


def kept_z():
    y, core, part, xl, k = np.meshgrid(
        np.arange(4), np.arange(2), np.arange(2), np.arange(2), np.arange(4), indexing="ij"
    )
    return (((y * 2 + xl) * 2 + core) * 4 + k).reshape(-1), part.reshape(-1)


def z_table():
    frequency, part = kept_z()
    angle = angles(frequency, np.arange(Z), Z)
    return np.where(part[:, None] == 0, np.cos(angle), -np.sin(angle)) * Z**-0.5


def rotation(angle, row_part, column_part, sign):
    same = row_part[:, None] == column_part[None, :]
    lower = row_part[:, None] > column_part[None, :]
    return np.where(same, np.cos(angle), np.where(lower, sign, -sign) * np.sin(angle))


def y_points(xl):
    y, core, point, part = np.meshgrid(
        np.arange(4), np.arange(2), np.arange(16), np.arange(2), indexing="ij"
    )
    return (((y * 2 + xl) * 2 + core) * 16 + point).reshape(-1), part.reshape(-1)


def z_table_rows(order):
    half, part, place, k = np.meshgrid(
        np.arange(2), np.arange(2), np.arange(8), np.arange(4), indexing="ij"
    )
    frequency = np.array(order)[half * 8 + place] * 4 + k
    angle = angles(frequency.reshape(-1), np.arange(Z), Z)
    return np.where(part.reshape(-1, 1) == 0, np.cos(angle), -np.sin(angle)) * Z**-0.5


def y_forward_rows(places):
    block, part, point = np.meshgrid(
        np.array(places), np.arange(2), np.arange(16), indexing="ij"
    )
    frequency, row_part = y_modes()
    angle = angles(frequency, (block * 16 + point).reshape(-1), Y)
    return rotation(angle, row_part, part.reshape(-1), -1) * Y**-0.5


def y_modes():
    block, part, j = np.meshgrid(np.arange(8), np.arange(2), np.arange(8), indexing="ij")
    return (block * 8 + j).reshape(-1) - MY // 2, part.reshape(-1)


def y_forward(xl):
    position, column_part = y_points(xl)
    frequency, row_part = y_modes()
    return rotation(angles(frequency, position, Y), row_part, column_part, -1) * Y**-0.5


def y_inverse(xl):
    position, row_part = y_points(xl)
    frequency, column_part = y_modes()
    return rotation(angles(frequency, position, Y).T, row_part, column_part, 1) * Y**-0.5


def x_points():
    return np.repeat(np.arange(X), 2), np.tile(np.arange(2), X)


def x_modes():
    return np.tile(np.arange(MX), 2) - MX // 2, np.repeat(np.arange(2), MX)


def x_forward():
    position, column_part = x_points()
    frequency, row_part = x_modes()
    return rotation(angles(frequency, position, X), row_part, column_part, -1) * X**-0.5


def x_inverse():
    position, row_part = x_points()
    frequency, column_part = x_modes()
    return rotation(angles(frequency, position, X).T, row_part, column_part, 1) * X**-0.5


def stacked(table):
    return np.concatenate(split_parts(table), 0)


def swap_table():
    index = np.arange(256)
    table = np.zeros((256, 256), ml_dtypes.bfloat16)
    table[index, (index % 16) * 16 + index // 16] = 1
    return table


def dot(a, b):
    return jnp.dot(a, b, preferred_element_type=F32)


def halves(values):
    high = values.astype(BF16)
    return high, (values - high.astype(F32)).astype(BF16)


def table_dot(table, values):
    rows = table.shape[0] // 2
    high, low = halves(values)
    both = dot(table, high)
    return both[:rows] + both[rows:] + dot(table[:rows], low)


def swap_quads(tiles):
    lane = lax.broadcasted_iota(jnp.int32, tiles[0].shape, 1) // 32
    result = []
    for b in range(4):
        total = None
        for a in range(4):
            shift = (32 * (a - b)) % 128
            moved = pltpu.roll(tiles[a], shift, 1) if shift else tiles[a]
            total = moved if total is None else jnp.where(lane == a, moved, total)
        result.append(total)
    return result


def by_source(refs):
    crossed = refs[4]
    return [crossed.at[i, 0] if j else refs[i].at[0, 0] for i in range(4) for j in range(2)]


def z_forward_kernel(volume, swap, table, *refs):
    out, rows = refs[:4], refs[4]
    for x in range(4):
        for half in range(2):
            block = volume[half * 16 : half * 16 + 16, x].reshape(256, Z)
            moved = dot(swap[...], block).astype(BF16)
            for y in range(16):
                rows[y, x, half * 16 : half * 16 + 16, :] = moved[y * 16 : y * 16 + 16]
    for pair in range(8):
        points = rows[pair * 2 : pair * 2 + 2].reshape(256, Z)
        both = lax.dot_general(
            table[...], points, (((1,), (1,)), ((), ())), preferred_element_type=F32
        )
        values = both[:128] + both[128:]
        for y in range(2):
            for target in range(8):
                for part in range(2):
                    row = (target * 2 + part) * 8
                    out[target // 2][target % 2, 0, pair * 2 + y, part] = values[
                        row : row + 8, y * 128 : y * 128 + 128
                    ]


def y_forward_kernel(*refs):
    received, table, out = by_source(refs[:5]), refs[5], refs[6]
    for quad in range(2):
        columns = []
        for k in range(4):
            kz = quad * 4 + k
            columns.append(
                jnp.concatenate(
                    [received[s][pl.ds(kz, 32, stride=8), :] for s in range(8)], 0
                )
            )
        values = table_dot(table[...], jnp.concatenate(columns, 1))
        tiles = swap_quads([values[:, k * 128 : k * 128 + 128] for k in range(4)])
        for x in range(4):
            for block in range(8):
                for part in range(2):
                    row = (block * 2 + part) * 8
                    out[block * 2 + quad, x, part] = tiles[x][row : row + 8]


def x_forward_kernel(received, table, out, flat):
    for ky in range(8):
        pieces = []
        for block in range(8):
            first = received[block * 2, pl.ds(ky, 32, stride=8), :]
            second = received[block * 2 + 1, pl.ds(ky, 32, stride=8), :]
            pieces.append(first + second)
        values = table_dot(table[...], jnp.concatenate(pieces, 0))
        for part in range(2):
            flat[2 + part, ky * 32 : ky * 32 + 32] = values[part * 32 : part * 32 + 32]
    for part in range(2):
        for high in range(2):
            turned = flat[2 + part, high * 128 : high * 128 + 128].T
            tiles = swap_quads([turned[k * 32 : k * 32 + 32] for k in range(4)])
            for low in range(4):
                row = (high * 4 + low) * 32
                flat[part, row : row + 32] = tiles[low]
        for c in range(C):
            out[part, c] = flat[part, pl.ds(c, 8, stride=32), :]


def z_forward_rows_kernel(volume, table, out):
    lower = lax.broadcasted_iota(jnp.int32, (64, 128), 1) < 64
    for x in range(4):
        for half in range(2):
            block = volume[half * 16 : half * 16 + 16, x].reshape(256, Z)
            both = lax.dot_general(
                table[...], block, (((1,), (1,)), ((), ())), preferred_element_type=F32
            )
            values = both[:128] + both[128:]
            for pair in range(2):
                tile = values[:, pair * 128 : pair * 128 + 128]
                first, second = tile[:64], tile[64:]
                results = (
                    jnp.where(lower, first, pltpu.roll(second, 64, 1)),
                    jnp.where(lower, pltpu.roll(first, 64, 1), second),
                )
                for e in range(2):
                    target = half * 4 + pair * 2 + e
                    for part in range(2):
                        for group in range(4):
                            row = (part * 4 + group) * 8
                            out[target, group, x, part] = results[e][row : row + 8]


def x_forward_rows_kernel(received, table, out):
    for quad in range(2):
        columns = []
        for k in range(4):
            columns.append(
                jnp.concatenate(
                    [received[s, 0, pl.ds(quad * 4 + k, 32, stride=8), :] for s in range(8)], 0
                )
            )
        values = table_dot(table[...], jnp.concatenate(columns, 1))
        for pair in range(2):
            stack = [values[:, k * 128 : k * 128 + 128] for k in (2 * pair, 2 * pair + 1)]
            turned = jnp.concatenate(stack, 0).T
            for p in range(2):
                rows = [p * 64 + c * 16 for c in range(4)]
                tiles = swap_quads([turned[row : row + 16] for row in rows])
                for k in range(2):
                    for part in range(2):
                        out[p, 0, quad, 2 * pair + k, part] = tiles[2 * k + part]


def y_forward_rows_kernel(*refs):
    received, table, out = refs[:4], refs[4], refs[5]
    for target in range(4):
        columns = []
        for k in range(4):
            rows = slice(k * 32, k * 32 + 32)
            columns.append(jnp.concatenate([received[s][target, rows] for s in range(4)], 0))
        values = table_dot(table[...], jnp.concatenate(columns, 1))
        for k in range(4):
            out[target, k] = values[:, k * 128 : k * 128 + 128]


def sum_rows_kernel(place, *refs):
    received, out = refs[:4], refs[4]
    for target in range(8):
        offset = (target % 4 + 4 - place[1]) % 4 * 2 + (target // 4 + 2 - place[0]) % 2
        for k in range(4):
            rows = slice(target * 16, target * 16 + 16)
            total = (received[0][k, rows] + received[1][k, rows]) + (
                received[2][k, rows] + received[3][k, rows]
            )
            out[offset, k] = total.reshape(2, 8, 128)


def mix_kernel(weight, spectra, out):
    for o in range(0, 8, 4):
        rows = slice(o * 8, o * 8 + 32)

        def step(c, totals):
            real, imag = totals
            weight_real = weight[0, c, rows].astype(F32)
            weight_imag = weight[1, c, rows].astype(F32)
            field_real = jnp.concatenate([spectra[0, c]] * 4, 0)
            field_imag = jnp.concatenate([spectra[1, c]] * 4, 0)
            real = real + weight_real * field_real - weight_imag * field_imag
            imag = imag + weight_real * field_imag + weight_imag * field_real
            return real, imag

        zero = jnp.zeros((32, 128), F32)
        real, imag = lax.fori_loop(0, C, step, (zero, zero), unroll=4)
        out[0, rows] = real
        out[1, rows] = imag


def back_kernel(*refs):
    place, weight, mixed, partner = refs[:4]
    arrived, crossed, back, cotangent = refs[4:8], refs[8], refs[9], refs[10]
    factor = math.sqrt(X * Y * Z / (MX * MY * MZ))

    @pl.when(pl.program_id(0) == 0)
    def _():
        for part in range(2):
            for offset in range(8):
                i, j = offset // 2, offset % 2
                source = (place[0] + j) % 2 * 4 + (place[1] + 4 - i) % 4
                target = crossed.at[i] if j else arrived[i].at[0]
                tiles = swap_quads([target[k, part] for k in range(4)])
                for c in range(4):
                    rows = pl.ds(pl.multiple_of(source * 32 + c * 8, 8), 8)
                    cotangent[part, rows] = (0.5 * factor * factor) * (
                        mixed[part, rows] + partner[part, rows]
                    ) - factor * tiles[c]

    def step(c, carry):
        real = jnp.zeros((32, 128), F32)
        imag = jnp.zeros((32, 128), F32)
        for o in range(0, C, 4):
            rows = slice(o * 8, o * 8 + 32)
            weight_real = weight[0, c, rows].astype(F32)
            weight_imag = weight[1, c, rows].astype(F32)
            real = real + weight_real * cotangent[0, rows] + weight_imag * cotangent[1, rows]
            imag = imag + weight_real * cotangent[1, rows] - weight_imag * cotangent[0, rows]
        back[0, c] = real[:8] + real[8:16] + real[16:24] + real[24:]
        back[1, c] = imag[:8] + imag[8:16] + imag[16:24] + imag[24:]
        return carry

    lax.fori_loop(0, 8, step, 0)


def x_inverse_kernel(back, table, first, second, flat):
    for part in range(2):
        for c in range(C):
            flat[part, pl.ds(c, 8, stride=32), :] = back[part, c]
    for high in range(2):
        turned = []
        for part in range(2):
            rows = [(high * 4 + low) * 32 for low in range(4)]
            tiles = swap_quads([flat[part, row : row + 32] for row in rows])
            turned.append(jnp.concatenate(tiles, 0).T)
        for low in range(4):
            ky = high * 4 + low
            modes = jnp.concatenate([t[low * 32 : low * 32 + 32] for t in turned], 0)
            values = table_dot(table[...], modes)
            for block in range(8):
                row = block * 32
                for xl in range(2):
                    first[block * 2 + xl, pl.ds(ky, 16, stride=8), :] = values[row : row + 16]
                    second[block * 2 + xl, pl.ds(ky, 16, stride=8), :] = values[
                        row + 16 : row + 32
                    ]


def y_inverse_kernel(received, table, *out):
    for quad in range(2):
        tiles = []
        for x in range(4):
            tiles.append(
                jnp.concatenate(
                    [received[block * 2 + quad, x].reshape(16, 128) for block in range(8)], 0
                )
            )
        columns = swap_quads(tiles)
        values = table_dot(table[...], jnp.concatenate(columns, 1))
        for k in range(4):
            for target in range(8):
                out[target // 2][target % 2, 0, pl.ds(quad * 4 + k, 32, stride=8), :] = values[
                    target * 32 : target * 32 + 32, k * 128 : k * 128 + 128
                ]


def z_inverse_kernel(*refs):
    received, swap, table, out, rows = by_source(refs[:5]), *refs[5:7], *refs[-2:]
    for y in range(16):
        modes = jnp.concatenate([received[s][y].reshape(16, 128) for s in range(8)], 0)
        high, low = halves(modes.T)
        both = jnp.concatenate([high, low], 1)
        first = jnp.concatenate([table[:128], table[:128]], 0)
        values = dot(both, first) + dot(high, table[128:])
        rows[y] = values.astype(BF16).reshape(4, 32, Z)
    for x in range(4):
        for half in range(2):
            block = jnp.concatenate(
                [rows[y, x, half * 16 : half * 16 + 16, :] for y in range(16)], 0
            )
            moved = dot(swap[...], block).astype(BF16)
            out[half * 16 : half * 16 + 16, x] = moved.reshape(16, 16, Z)


SCALARS = pl.BlockSpec(memory_space=pltpu.SMEM)


def row_place():
    return jnp.stack([lax.axis_index("xh"), lax.axis_index("z")]).astype(jnp.int32)


def call(kernel, out, grid, in_specs, out_specs, scratch=(), cost=None, grant=40):
    return pl.pallas_call(
        kernel,
        out_shape=out,
        grid=grid,
        in_specs=in_specs,
        out_specs=out_specs,
        scratch_shapes=list(scratch),
        compiler_params=pltpu.CompilerParams(vmem_limit_bytes=grant * 2**20),
        cost_estimate=cost,
    )


def whole(*dims):
    return pl.BlockSpec(dims, lambda *i: (0,) * len(dims))


def struct(*dims, kind=F32):
    return jax.ShapeDtypeStruct(dims, kind)


def estimate(flops, moved):
    return pl.CostEstimate(flops=flops, bytes_accessed=moved, transcendentals=0)


def z_forward_call(volume, table):
    return call(
        z_forward_kernel,
        [struct(2, 4, 16, 2, 8, 128)] * 4,
        (4,),
        [
            pl.BlockSpec((32, 4, 16, Z), lambda i: (0, i, 0, 0)),
            whole(256, 256),
            whole(256, Z),
        ],
        [pl.BlockSpec((2, 1, 16, 2, 8, 128), lambda i: (0, i, 0, 0, 0, 0))] * 4,
        [pltpu.VMEM((16, 4, 32, Z), BF16)],
        estimate(3 * 2**30, 8 * 2**20),
        60,
    )(volume, jnp.asarray(swap_table()), table)


def y_forward_call(received, table):
    return call(
        y_forward_kernel,
        struct(16, 16, 2, 8, 128),
        (4,),
        [pl.BlockSpec((1, 1, 256, 128), lambda i: (0, i, 0, 0))] * 4
        + [pl.BlockSpec((4, 1, 256, 128), lambda i: (0, i, 0, 0)), whole(256, 256)],
        pl.BlockSpec((16, 4, 2, 8, 128), lambda i: (0, i, 0, 0, 0)),
        (),
        estimate(2 * 2**30, 6 * 2**20),
    )(*[block.reshape(block.shape[:-4] + (256, 128)) for block in received], table)


def z_forward_rows_call(volume, table):
    return call(
        z_forward_rows_kernel,
        struct(8, 4, 16, 2, 8, 128),
        (4,),
        [
            pl.BlockSpec((32, 4, 16, Z), lambda i: (0, i, 0, 0)),
            whole(256, Z),
        ],
        pl.BlockSpec((8, 4, 4, 2, 8, 128), lambda i: (0, 0, i, 0, 0, 0)),
        (),
        estimate(2 * 2**30, 8 * 2**20),
        60,
    )(volume, table)


def x_forward_rows_call(received):
    return call(
        x_forward_rows_kernel,
        struct(2, 4, 2, 4, 2, 16, 128),
        (4,),
        [
            pl.BlockSpec((8, 1, 256, 128), lambda i: (0, i, 0, 0)),
            whole(128, 256),
        ],
        pl.BlockSpec((2, 1, 2, 4, 2, 16, 128), lambda i: (0, i, 0, 0, 0, 0, 0)),
        (),
        estimate(2**20, 2**16),
    )(received.reshape(8, 4, 256, 128), jnp.asarray(stacked(x_forward())))


def y_forward_rows_call(received, table):
    return call(
        y_forward_rows_kernel,
        struct(4, 4, 128, 128),
        (),
        [whole(4, 128, 128)] * 4 + [whole(256, 128)],
        whole(4, 4, 128, 128),
        (),
        estimate(2**20, 2**16),
    )(*received, table)


def sum_rows_call(received):
    return call(
        sum_rows_kernel,
        struct(8, 4, 2, 8, 128),
        (),
        [SCALARS] + [whole(4, 128, 128)] * 4,
        whole(8, 4, 2, 8, 128),
        (),
        estimate(2**20, 2**16),
    )(row_place(), *received)


def x_forward_call(received):
    return call(
        x_forward_kernel,
        struct(2, 32, 8, 128),
        (),
        [whole(16, 256, 128), whole(128, 256)],
        whole(2, 32, 8, 128),
        [pltpu.VMEM((4, 256, 128), F32)],
        estimate(2**28, 3 * 2**20),
    )(received.reshape(16, 256, 128), jnp.asarray(stacked(x_forward())))


def mix_call(weight, spectra):
    return call(
        mix_kernel,
        struct(2, 256, 128),
        (4,),
        [
            pl.BlockSpec((2, 32, 64, 128), lambda i: (0, 0, i, 0)),
            whole(2, 32, 8, 128),
        ],
        pl.BlockSpec((2, 64, 128), lambda i: (0, i, 0)),
        (),
        estimate(2**27, 5 * 2**20),
    )(weight, spectra)


def back_call(weight, mixed, partner, target):
    small = whole(2, 256, 128)
    return call(
        back_kernel,
        (struct(2, 32, 8, 128), struct(2, 256, 128)),
        (4,),
        [
            SCALARS,
            pl.BlockSpec((2, 8, 256, 128), lambda i: (0, i, 0, 0)),
            small,
            small,
        ]
        + [whole(2, 4, 2, 8, 128)] * 4
        + [whole(4, 4, 2, 8, 128)],
        (pl.BlockSpec((2, 8, 8, 128), lambda i: (0, i, 0, 0)), small),
        (),
        estimate(2**27, 5 * 2**20),
    )(row_place(), weight, mixed, partner, *target)


def x_inverse_call(back):
    return call(
        x_inverse_kernel,
        [struct(16, 128, 128)] * 2,
        (),
        [whole(2, 32, 8, 128), whole(512, 64)],
        [whole(16, 128, 128)] * 2,
        [pltpu.VMEM((2, 256, 128), F32)],
        estimate(2**28, 3 * 2**20),
    )(back, jnp.asarray(stacked(x_inverse())))


def y_inverse_call(received, table):
    return call(
        y_inverse_kernel,
        [struct(2, 2, 256, 128)] * 4,
        (2,),
        [
            pl.BlockSpec((16, 4, 2, 8, 128), lambda i: (0, i, 0, 0, 0)),
            whole(512, 128),
        ],
        [pl.BlockSpec((2, 1, 256, 128), lambda i: (0, i, 0, 0))] * 4,
        (),
        estimate(2**30, 3 * 2**20),
    )(received.reshape(16, 8, 2, 8, 128), table)


def z_inverse_call(received, table, half, others):
    return pl.pallas_call(
        z_inverse_kernel,
        out_shape=struct(32, 16, 16, Z, kind=BF16),
        grid=(2,),
        in_specs=[pl.BlockSpec((1, 1, 16, 2, 8, 128), lambda i: (0, i, 0, 0, 0, 0))] * 4
        + [pl.BlockSpec((4, 1, 16, 2, 8, 128), lambda i: (0, i, 0, 0, 0, 0))]
        + [whole(256, 256), whole(256, Z)]
        + [pl.BlockSpec(memory_space=pl.ANY)] * len(others),
        out_specs=pl.BlockSpec((32, 4, 16, Z), lambda i: (0, i + 2 * half, 0, 0)),
        scratch_shapes=[pltpu.VMEM((16, 4, 32, Z), BF16)],
        input_output_aliases={7: 0} if others else {},
        compiler_params=pltpu.CompilerParams(vmem_limit_bytes=40 * 2**20),
        cost_estimate=estimate(3 * 2**29, 4 * 2**20),
    )(
        *[block.reshape(block.shape[:-2] + (16, 2, 8, 128)) for block in received],
        jnp.asarray(swap_table()),
        table,
        *others,
    )


def exchange(values, axes):
    return lax.all_to_all(values, axes, split_axis=0, concat_axis=0, tiled=True)


def offset_pairs(offset):
    index = np.arange(math.prod(SHAPE))
    place = np.stack(np.unravel_index(index, SHAPE))
    other = (place + np.array(offset)[:, None]) % np.array(SHAPE)[:, None]
    return list(zip(index.tolist(), np.ravel_multi_index(other, SHAPE).tolist()))


def shifted(values, **steps):
    offset = [steps.get(a, 0) for a in AXES]
    return lax.ppermute(values, AXES, offset_pairs(offset)) if any(offset) else values


def cross(arrived):
    return arrived + [shifted(jnp.stack([block[1] for block in arrived]), core=1)]


def by_place(build):
    tables = np.stack(
        [build(y, core, xl) for y in range(4) for core in range(2) for xl in range(2)]
    )
    y, core, xl = (lax.axis_index(a) for a in ("y", "core", "xl"))
    return lax.dynamic_index_in_dim(
        jnp.asarray(tables), (y * 2 + core) * 2 + xl, 0, keepdims=False
    )


def first_order(y, core, sign):
    return [((y + sign * i) % 4) * 2 + (core + sign * j) % 2 for i in range(4) for j in range(2)]


def z_rows_by_offset(y, core, xl):
    table = z_table().reshape(8, 16, Z)[first_order(y, core, 1)]
    return stacked(table.reshape(128, Z))


def z_rows_by_col(y, core, xl):
    order = [
        (((y + i) % 4) * 2 + (xl + j) % 2) * 2 + (core + k) % 2
        for i in range(4)
        for j in range(2)
        for k in range(2)
    ]
    return stacked(z_table_rows(order))


def y_columns_by_col(y, core, xl):
    return stacked(y_forward_rows([((y - i) % 4 * 2 + xl) * 2 + core for i in range(4)]))


def z_rows_by_source(y, core, xl):
    table = z_table().reshape(8, 16, Z)[first_order(y, core, -1)]
    return stacked(table.reshape(128, Z))


def y_rows_by_offset(y, core, xl):
    table = y_inverse(xl).reshape(8, 32, 128)[first_order(y, core, 1)]
    return stacked(table.reshape(256, 128))


def y_columns_by_offset(y, core, xl):
    table = y_forward(xl).reshape(128, 8, 32)[:, first_order(y, core, -1)]
    return stacked(table.reshape(128, 256))


def plane_pairs():
    index = np.arange(math.prod(SHAPE)).reshape(8, 16)[:, 0].tolist()
    same = [(index[b], index[7 - b]) for b in range(8)]
    edge = [(index[b], index[8 - b]) for b in range(1, 8)]
    return same, edge


def mirrored(mixed):
    same_pairs, edge_pairs = plane_pairs()
    plane = mixed.reshape(2, C, 8, 128)[..., :MX]
    same = lax.ppermute(plane, AXES, same_pairs)
    edge = lax.ppermute(plane[:, :, :1], AXES, edge_pairs)
    by_ky = jnp.concatenate([edge, same[:, :, :0:-1]], 2)
    by_kx = jnp.concatenate([jnp.zeros_like(by_ky[..., :1]), by_ky[..., :0:-1]], 3)
    signed = by_kx * jnp.array([1.0, -1.0], F32)[:, None, None, None]
    padded = jnp.pad(signed, ((0, 0),) * 3 + ((0, 128 - MX),))
    return padded.reshape(2, 256, 128)


def weight_grad(spectra, cotangent):
    real, imag = spectra.reshape(2, 1, C, 1, 8, 4, MX)
    turned = jnp.stack([cotangent[1], -cotangent[0]])
    cotangent, turned = (a.reshape(2, 1, C, 8, 4, MX) for a in (cotangent, turned))
    return (real * cotangent + imag * turned).astype(BF16)


def per_device(voxels, target, weight):
    barrier = lax.optimization_barrier
    packed = weight.reshape(2, C, 256, 128)

    target_lines = z_forward_rows_call(target, by_place(z_rows_by_col))
    target_lines, voxels = barrier((target_lines, voxels))
    target_lines = exchange(target_lines, ROW)
    lines = z_forward_call(voxels, by_place(z_rows_by_offset))
    lines = [shifted(block, y=i) for i, block in enumerate(lines)]
    target_lines, packed = barrier((target_lines, packed))
    blocks = x_forward_rows_call(target_lines).reshape(4, 4, 128, 128)
    lines, blocks = barrier((lines, blocks))
    blocks = [shifted(blocks[i], y=i) for i in range(4)]
    planes = y_forward_call(cross(lines), by_place(y_columns_by_offset))
    planes, blocks = barrier((planes, blocks))
    planes = exchange(planes, SECOND)
    blocks = y_forward_rows_call(blocks, by_place(y_columns_by_col))
    blocks = [shifted(blocks[2 * i + j], xl=i, core=j) for i in range(2) for j in range(2)]
    spectra = x_forward_call(planes)
    mixed = mix_call(packed, spectra)
    mixed, blocks = barrier((mixed, blocks))
    arrived = sum_rows_call(blocks)
    arrived = [shifted(arrived[2 * i : 2 * i + 2], z=i) for i in range(4)]
    partner, arrived = barrier((mirrored(mixed), arrived))
    crossed = shifted(jnp.stack([block[1] for block in arrived]), xh=1)
    back, cotangent = back_call(packed, mixed, partner, arrived + [crossed])
    y_table, z_table_here = by_place(y_rows_by_offset), by_place(z_rows_by_source)
    first, second = x_inverse_call(back)
    first, second = barrier((exchange(first, SECOND), second))
    first = y_inverse_call(first, y_table)
    first = [shifted(block, y=i) for i, block in enumerate(first)]
    second = y_inverse_call(exchange(second, SECOND), y_table)
    second = [shifted(block, y=i) for i, block in enumerate(second)]
    grad = weight_grad(spectra, cotangent)
    first, grad = barrier((first, grad))
    field = z_inverse_call(cross(first), z_table_here, 0, [])
    second, field = barrier((second, field))
    return z_inverse_call(cross(second), z_table_here, 1, [field]), grad


def solution(mesh):
    fine = Mesh(mesh.devices.reshape(SHAPE), AXES)
    field = P(None, ROW, COL, None)
    modes = P(None, None, None, ROW, COL, None)
    return jax.shard_map(
        per_device,
        mesh=fine,
        in_specs=(field, field, modes),
        out_specs=(field, modes),
        check_vma=False,
    )
```

profile of v0, /device:TPU:1, one launch (start us, length us, event | category | flops | bytes accessed | tf_op | source)
XLA Modules:
  0.0 253.3 jit_solution(13393031360752739440)
XLA Ops:
  2.3 5.8 %shard_map.167 = f32[8,4,16,2,8,128]{5,4,3,2,1,0:T(8,128)} custom-call(bf16[32,16,16,256]{3,2,1,0:T(8,128)(2,1)} %volume.1, bf16[256,256]{1,0:T(8,128)(2,1)} %get-tuple-element.123.table), custom_call_target="tpu_custom_call" | custom-call | flops 2147483648 | bytes 8388608 | tf_op jit(solution)/shard_map/pallas_call | solution.py:478
  8.1 8.3 %all-to-all-start = ((f32[8,4,16,2,8,128]{5,4,3,2,1,0:T(8,128)}), f32[8,4,16,2,8,128]{5,4,3,2,1,0:T(8,128)}, u32[]{:S(2)}, u32[]{:S(2)}) async-start(f32[8,4,16,2,8,128]{5,4,3,2,1,0:T(8,128)} %shard_map.167), calls=%async_computation | async-start | bytes 8388608 | tf_op jit(solution)/shard_map/all_to_all | solution.py:629
  16.5 6.6 %shard_map.168 = (f32[2,4,16,2,8,128]{5,4,3,2,1,0:T(8,128)}, f32[2,4,16,2,8,128]{5,4,3,2,1,0:T(8,128)}, f32[2,4,16,2,8,128]{5,4,3,2,1,0:T(8,128)}, f32[2,4,16,2,8,128]{5,4,3,2,1,0:T(8,128)}) custom-call(bf16[32,16,16,256]{3,2,1,0:T(8,128)(2,1)} %volume.2, bf16[256,256]{1,0:T(8,128)(2,1)} %constant.67.clone.swap.refs_5_, ...), custom_call_target="tpu_custom_call" | custom-call | flops 3221225472 | bytes 8388608 | tf_op jit(solution)/shard_map/pallas_call | solution.py:448
  24.3 2.6 %collective-permute-start.1 = (f32[2,4,16,2,8,128]{5,4,3,2,1,0:T(8,128)}, f32[2,4,16,2,8,128]{5,4,3,2,1,0:T(8,128)S(1)}, u32[]{:S(2)}, u32[]{:S(2)}) collective-permute-start(f32[2,4,16,2,8,128]{5,4,3,2,1,0:T(8,128)} %get-tuple-element.59), channel_id=1, source_target_pairs={{0,8},{1,9},{2,10},{3,11},{4,12},{5,13},{6,14},{7,15},{8,0},{9,1},... | collective-permute-start | bytes 3145736 | tf_op jit(solution)/shard_map/ppermute | solution.py:641
  28.0 19.9 %reshape.86.weight.refs_1_ = bf16[2,32,256,128]{3,2,1,0:T(8,128)(2,1)} reshape(bf16[2,32,32,8,4,32]{5,4,3,2,1,0:T(4,128)(2,1)} %param.18) | data formatting | bytes 8388608 | tf_op jit(solution)/shard_map/reshape | solution.py:724
  48.0 17.2 %all-to-all-done = f32[8,4,16,2,8,128]{5,4,3,2,1,0:T(8,128)} async-done(((f32[8,4,16,2,8,128]{5,4,3,2,1,0:T(8,128)}), f32[8,4,16,2,8,128]{5,4,3,2,1,0:T(8,128)}, u32[]{:S(2)}, u32[]{:S(2)}) %all-to-all-start) | async-done | bytes 4194336 | tf_op jit(solution)/shard_map/all_to_all | solution.py:629
  65.2 5.0 %shard_map.169 = f32[2,4,2,4,2,16,128]{6,5,4,3,2,1,0:T(8,128)S(1)} custom-call(f32[8,4,256,128]{3,2,1,0:T(8,128)} %bitcast.4.received, bf16[128,256]{1,0:T(8,128)(2,1)S(1)} %copy-done.11), custom_call_target="tpu_custom_call" | custom-call | flops 1048576 | bytes 65536 | tf_op jit(solution)/shard_map/pallas_call | solution.py:494
  78.4 3.6 %shard_map.170 = f32[16,16,2,8,128]{4,3,2,1,0:T(8,128)S(1)} custom-call(f32[2,4,256,128]{3,2,1,0:T(8,128)S(1)} %bitcast.62, f32[2,4,256,128]{3,2,1,0:T(8,128)S(1)} %bitcast.63, f32[2,4,256,128]{3,2,1,0:T(8,128)S(1)} %bitcast.64, f32[2,4,256,128]{3,2,1,0:T(8,128)S(1)} %bitcast.65, f32[4,4,256,128]{3,2,1,0:T(8,128)S(1)} %bitcast.66, ...), custom_call_target="tpu_custom_call" | custom-call | flops 2147483648 | bytes 6291456 | tf_op jit(solution)/shard_map/pallas_call | solution.py:465
  86.1 5.5 %collective-permute-done.4.refs_1_ = f32[4,128,128]{2,1,0:T(8,128)S(1)} collective-permute-done((f32[4,128,128]{2,1,0:T(8,128)S(1)}, f32[4,128,128]{2,1,0:T(8,128)S(1)}, u32[]{:S(2)}, u32[]{:S(2)}) %collective-permute-start.4) | collective-permute-done | bytes 262176 | tf_op jit(solution)/shard_map/ppermute | solution.py:641
  92.3 6.9 %all-to-all-start.1 = ((f32[16,16,2,8,128]{4,3,2,1,0:T(8,128)}), f32[16,16,2,8,128]{4,3,2,1,0:T(8,128)S(1)}, u32[]{:S(2)}, u32[]{:S(2)}) async-start(f32[16,16,2,8,128]{4,3,2,1,0:T(8,128)} %copy-done.2), calls=%async_computation.1 | async-start | bytes 4194304 | tf_op jit(solution)/shard_map/all_to_all | solution.py:629
  104.3 25.0 %all-to-all-done.1 = f32[16,16,2,8,128]{4,3,2,1,0:T(8,128)S(1)} async-done(((f32[16,16,2,8,128]{4,3,2,1,0:T(8,128)}), f32[16,16,2,8,128]{4,3,2,1,0:T(8,128)S(1)}, u32[]{:S(2)}, u32[]{:S(2)}) %all-to-all-start.1) | async-done | bytes 2097184 | tf_op jit(solution)/shard_map/all_to_all | solution.py:629
  137.2 5.0 %collective-permute-start.14 = (f32[2,4,2,8,128]{4,3,2,1,0:T(8,128)S(1)}, f32[2,4,2,8,128]{4,3,2,1,0:T(8,128)S(1)}, u32[]{:S(2)}, u32[]{:S(2)}) collective-permute-start(f32[2,4,2,8,128]{4,3,2,1,0:T(8,128)S(1)} %get-tuple-element.118), channel_id=1, source_target_pairs={{0,48},{1,49},{2,50},{3,51},{4,52},{5,53},{6,54},{7,55},{8,56},{9,... | collective-permute-start | bytes 196616 | tf_op jit(solution)/shard_map/ppermute | solution.py:641
  149.9 4.9 %collective-permute-done.15.refs_8_ = f32[4,4,2,8,128]{4,3,2,1,0:T(8,128)S(1)} collective-permute-done((f32[4,4,2,8,128]{4,3,2,1,0:T(8,128)S(1)}, f32[4,4,2,8,128]{4,3,2,1,0:T(8,128)S(1)}, u32[]{:S(2)}, u32[]{:S(2)}) %collective-permute-start.15) | collective-permute-done | bytes 131104 | tf_op jit(solution)/shard_map/ppermute | solution.py:641
  157.0 3.0 %shard_map.175 = (f32[2,32,8,128]{3,2,1,0:T(8,128)S(1)}, f32[2,256,128]{2,1,0:T(8,128)S(1)}) custom-call(s32[2]{0:T(128)S(1)} %pad_add_fusion.place.refs_0_, bf16[2,32,256,128]{3,2,1,0:T(8,128)(2,1)S(1)} %copy-done.1, f32[2,256,128]{2,1,0:T(8,128)S(1)} %shard_map.172.refs_2_, f32[2,256,128]{2,1,0:T(8,128)S(1)} %pad_bitcast_fusion.refs_3_, ...), custom_call_target="tpu_custom_call" | custom-call | flops 134217728 | bytes 5242880 | tf_op jit(solution)/shard_map/pallas_call | solution.py:561
  162.4 4.6 %all-to-all-start.2 = ((f32[16,128,128]{2,1,0:T(8,128)}), f32[16,128,128]{2,1,0:T(8,128)S(1)}, u32[]{:S(2)}, u32[]{:S(2)}) async-start(f32[16,128,128]{2,1,0:T(8,128)} %get-tuple-element.83), calls=%async_computation.2 | async-start | bytes 2097152 | tf_op jit(solution)/shard_map/all_to_all | solution.py:629
  173.4 5.8 %all-to-all-done.2 = f32[16,128,128]{2,1,0:T(8,128)S(1)} async-done(((f32[16,128,128]{2,1,0:T(8,128)}), f32[16,128,128]{2,1,0:T(8,128)S(1)}, u32[]{:S(2)}, u32[]{:S(2)}) %all-to-all-start.2) | async-done | bytes 1048608 | tf_op jit(solution)/shard_map/all_to_all | solution.py:629
  179.2 3.7 %all-to-all-start.3 = ((f32[16,128,128]{2,1,0:T(8,128)}), f32[16,128,128]{2,1,0:T(8,128)S(1)}, u32[]{:S(2)}, u32[]{:S(2)}) async-start(f32[16,128,128]{2,1,0:T(8,128)} %get-tuple-element.85), calls=%async_computation.3 | async-start | bytes 2097152 | tf_op jit(solution)/shard_map/all_to_all | solution.py:629
  184.9 5.0 %collective-permute-start.20 = (f32[2,2,256,128]{3,2,1,0:T(8,128)S(1)}, f32[2,2,256,128]{3,2,1,0:T(8,128)S(1)}, u32[]{:S(2)}, u32[]{:S(2)}) collective-permute-start(f32[2,2,256,128]{3,2,1,0:T(8,128)S(1)} %get-tuple-element.93), channel_id=1, source_target_pairs={{0,8},{1,9},{2,10},{3,11},{4,12},{5,13},{6,14},{7,15},{8,0},{9,1},... | collective-permute-start | bytes 1572872 | tf_op jit(solution)/shard_map/ppermute | solution.py:641
  191.8 12.5 %add_convert_fusion = bf16[2,32,32,8,4,32]{5,4,3,2,1,0:T(4,128)(2,1)} fusion(f32[2,32,8,4,32]{4,3,2,1,0:T(4,128)S(1)} %copy-done.14, f32[32,8,4,32]{3,2,1,0:T(4,128)S(1)} %copy-done.16, f32[2,32,8,4,32]{4,3,2,1,0:T(4,128)S(1)} %copy-done.13, f32[32,8,4,32]{3,2,1,0:T(4,128)S(1)} %copy-done.15), kind=kLoop, calls=%fused_computation | loop fusion | flops 8388608 | bytes 4980736 | tf_op jit(solution)/shard_map/convert_element_type | solution.py:719
  204.4 6.3 %collective-permute-done.20 = f32[2,2,256,128]{3,2,1,0:T(8,128)S(1)} collective-permute-done((f32[2,2,256,128]{3,2,1,0:T(8,128)S(1)}, f32[2,2,256,128]{3,2,1,0:T(8,128)S(1)}, u32[]{:S(2)}, u32[]{:S(2)}) %collective-permute-start.20) | collective-permute-done | bytes 524320 | tf_op jit(solution)/shard_map/ppermute | solution.py:641
  211.8 6.2 %collective-permute-start.22 = (f32[4,2,256,128]{3,2,1,0:T(8,128)}, f32[4,2,256,128]{3,2,1,0:T(8,128)}, u32[]{:S(2)}, u32[]{:S(2)}) collective-permute-start(f32[4,2,256,128]{3,2,1,0:T(8,128)} %pad_maximum_fusion.1), channel_id=1, source_target_pairs={{0,1},{1,0},{2,3},{3,2},{4,5},{5,4},{6,7},{7,6},{8,9},{9,8},{10,11... | collective-permute-start | bytes 3145736 | tf_op jit(solution)/shard_map/ppermute | solution.py:641
  223.6 4.3 %shard_map.179.refs_7_ = bf16[32,16,16,256]{3,2,1,0:T(8,128)(2,1)} custom-call(f32[2,2,16,2,8,128]{5,4,3,2,1,0:T(8,128)S(1)} %bitcast.73, f32[2,2,16,2,8,128]{5,4,3,2,1,0:T(8,128)S(1)} %bitcast.74, f32[2,2,16,2,8,128]{5,4,3,2,1,0:T(8,128)S(1)} %bitcast.75, f32[2,2,16,2,8,128]{5,4,3,2,1,0:T(8,128)S(1)} %bitcast.76, ...), custom_call_target="tpu_custom_call" | custom-call | flops 1610612736 | bytes 4194304 | tf_op jit(solution)/shard_map/pallas_call | solution.py:607
  227.9 18.0 %collective-permute-done.16 = f32[2,2,256,128]{3,2,1,0:T(8,128)S(1)} collective-permute-done((f32[2,2,256,128]{3,2,1,0:T(8,128)S(1)}, f32[2,2,256,128]{3,2,1,0:T(8,128)S(1)}, u32[]{:S(2)}, u32[]{:S(2)}) %collective-permute-start.16) | collective-permute-done | bytes 524320 | tf_op jit(solution)/shard_map/ppermute | solution.py:641
  249.9 3.4 %shard_map.180 = bf16[32,16,16,256]{3,2,1,0:T(8,128)(2,1)} custom-call(f32[2,2,16,2,8,128]{5,4,3,2,1,0:T(8,128)S(1)} %bitcast.69, f32[2,2,16,2,8,128]{5,4,3,2,1,0:T(8,128)S(1)} %bitcast.70, f32[2,2,16,2,8,128]{5,4,3,2,1,0:T(8,128)S(1)} %bitcast.71, f32[2,2,16,2,8,128]{5,4,3,2,1,0:T(8,128)S(1)} %bitcast.72, ...), custom_call_target="tpu_custom_call", output_to_operand_aliasing={{}: (7, {})} | custom-call | flops 1610612736 | bytes 4194304 | tf_op jit(solution)/shard_map/pallas_call | solution.py:607
  (128 shorter events, 63.0 us)
Async XLA Ops:
  8.1 57.1 %all-to-all-start = ((f32[8,4,16,2,8,128]{5,4,3,2,1,0:T(8,128)}), f32[8,4,16,2,8,128]{5,4,3,2,1,0:T(8,128)}, u32[]{:S(2)}, u32[]{:S(2)}) async-start(f32[8,4,16,2,8,128]{5,4,3,2,1,0:T(8,128)} %shard_map.167), calls=%async_computation | async-start | bytes 8388608 | tf_op jit(solution)/shard_map/all_to_all | solution.py:629
  23.1 47.1 %collective-permute-start = (f32[2,4,16,2,8,128]{5,4,3,2,1,0:T(8,128)}, f32[2,4,16,2,8,128]{5,4,3,2,1,0:T(8,128)S(1)}, u32[]{:S(2)}, u32[]{:S(2)}) collective-permute-start(f32[2,4,16,2,8,128]{5,4,3,2,1,0:T(8,128)} %get-tuple-element.58), channel_id=1, source_target_pairs={{0,4},{1,5},{2,6},{3,7},{4,8},{5,9},{6,10},{7,11},{8,12},{9,13},{1... | collective-permute-start | bytes 3145736 | tf_op jit(solution)/shard_map/ppermute | solution.py:641
  24.3 47.5 %collective-permute-start.1 = (f32[2,4,16,2,8,128]{5,4,3,2,1,0:T(8,128)}, f32[2,4,16,2,8,128]{5,4,3,2,1,0:T(8,128)S(1)}, u32[]{:S(2)}, u32[]{:S(2)}) collective-permute-start(f32[2,4,16,2,8,128]{5,4,3,2,1,0:T(8,128)} %get-tuple-element.59), channel_id=1, source_target_pairs={{0,8},{1,9},{2,10},{3,11},{4,12},{5,13},{6,14},{7,15},{8,0},{9,1},... | collective-permute-start | bytes 3145736 | tf_op jit(solution)/shard_map/ppermute | solution.py:641
  27.0 44.9 %collective-permute-start.2 = (f32[2,4,16,2,8,128]{5,4,3,2,1,0:T(8,128)}, f32[2,4,16,2,8,128]{5,4,3,2,1,0:T(8,128)S(1)}, u32[]{:S(2)}, u32[]{:S(2)}) collective-permute-start(f32[2,4,16,2,8,128]{5,4,3,2,1,0:T(8,128)} %get-tuple-element.60), channel_id=1, source_target_pairs={{0,12},{1,13},{2,14},{3,15},{4,0},{5,1},{6,2},{7,3},{8,4},{9,5},{1... | collective-permute-start | bytes 3145736 | tf_op jit(solution)/shard_map/ppermute | solution.py:641
  74.3 9.0 %collective-permute-start.6 = (f32[4,128,128]{2,1,0:T(8,128)S(1)}, f32[4,128,128]{2,1,0:T(8,128)S(1)}, u32[]{:S(2)}, u32[]{:S(2)}) collective-permute-start(f32[4,128,128]{2,1,0:T(8,128)S(1)} %get-tuple-element.110), channel_id=1, source_target_pairs={{0,12},{1,13},{2,14},{3,15},{4,0},{5,1},{6,2},{7,3},{8,4},{9,5},{1... | collective-permute-start | bytes 786440 | tf_op jit(solution)/shard_map/ppermute | solution.py:641
  76.2 9.2 %collective-permute-start.5 = (f32[4,128,128]{2,1,0:T(8,128)S(1)}, f32[4,128,128]{2,1,0:T(8,128)S(1)}, u32[]{:S(2)}, u32[]{:S(2)}) collective-permute-start(f32[4,128,128]{2,1,0:T(8,128)S(1)} %get-tuple-element.111), channel_id=1, source_target_pairs={{0,8},{1,9},{2,10},{3,11},{4,12},{5,13},{6,14},{7,15},{8,0},{9,1},... | collective-permute-start | bytes 786440 | tf_op jit(solution)/shard_map/ppermute | solution.py:641
  77.1 14.5 %collective-permute-start.4 = (f32[4,128,128]{2,1,0:T(8,128)S(1)}, f32[4,128,128]{2,1,0:T(8,128)S(1)}, u32[]{:S(2)}, u32[]{:S(2)}) collective-permute-start(f32[4,128,128]{2,1,0:T(8,128)S(1)} %get-tuple-element.112), channel_id=1, source_target_pairs={{0,4},{1,5},{2,6},{3,7},{4,8},{5,9},{6,10},{7,11},{8,12},{9,13},{1... | collective-permute-start | bytes 786440 | tf_op jit(solution)/shard_map/ppermute | solution.py:641
  92.3 37.1 %all-to-all-start.1 = ((f32[16,16,2,8,128]{4,3,2,1,0:T(8,128)}), f32[16,16,2,8,128]{4,3,2,1,0:T(8,128)S(1)}, u32[]{:S(2)}, u32[]{:S(2)}) async-start(f32[16,16,2,8,128]{4,3,2,1,0:T(8,128)} %copy-done.2), calls=%async_computation.1 | async-start | bytes 4194304 | tf_op jit(solution)/shard_map/all_to_all | solution.py:629
  101.5 33.1 %collective-permute-start.9 = (f32[4,128,128]{2,1,0:T(8,128)}, f32[4,128,128]{2,1,0:T(8,128)S(1)}, u32[]{:S(2)}, u32[]{:S(2)}) collective-permute-start(f32[4,128,128]{2,1,0:T(8,128)} %get-tuple-element.106), channel_id=1, source_target_pairs={{0,3},{1,2},{2,1},{3,0},{4,7},{5,6},{6,5},{7,4},{8,11},{9,10},{10,... | collective-permute-start | bytes 786440 | tf_op jit(solution)/shard_map/ppermute | solution.py:641
  103.8 31.4 %collective-permute-start.8 = (f32[4,128,128]{2,1,0:T(8,128)}, f32[4,128,128]{2,1,0:T(8,128)S(1)}, u32[]{:S(2)}, u32[]{:S(2)}) collective-permute-start(f32[4,128,128]{2,1,0:T(8,128)} %get-tuple-element.107), channel_id=1, source_target_pairs={{0,2},{1,3},{2,0},{3,1},{4,6},{5,7},{6,4},{7,5},{8,10},{9,11},{10,... | collective-permute-start | bytes 786440 | tf_op jit(solution)/shard_map/ppermute | solution.py:641
  103.8 31.4 %collective-permute-start.7 = (f32[4,128,128]{2,1,0:T(8,128)}, f32[4,128,128]{2,1,0:T(8,128)S(1)}, u32[]{:S(2)}, u32[]{:S(2)}) collective-permute-start(f32[4,128,128]{2,1,0:T(8,128)} %get-tuple-element.108), channel_id=1, source_target_pairs={{0,1},{1,0},{2,3},{3,2},{4,5},{5,4},{6,7},{7,6},{8,9},{9,8},{10,11... | collective-permute-start | bytes 786440 | tf_op jit(solution)/shard_map/ppermute | solution.py:641
  135.3 8.6 %collective-permute-start.10 = (f32[2,32,1,32]{3,2,1,0:T(1,128)S(1)}, f32[2,32,1,32]{3,2,1,0:T(1,128)S(1)}, u32[]{:S(2)}, u32[]{:S(2)}) collective-permute-start(f32[2,32,1,32]{3,2,1,0:T(1,128)S(1)} %slice.143), channel_id=1, source_target_pairs={{16,112},{32,96},{48,80},{64,64},{80,48},{96,32},{112,16}} | collective-permute-start | bytes 24584 | tf_op jit(solution)/shard_map/ppermute | solution.py:707
  135.9 7.8 %collective-permute-start.11 = (f32[2,32,8,32]{3,2,1,0:T(8,128)S(1)}, f32[2,32,8,32]{3,2,1,0:T(8,128)S(1)}, u32[]{:S(2)}, u32[]{:S(2)}) collective-permute-start(f32[2,32,8,32]{3,2,1,0:T(8,128)S(1)} %bitcast.68), channel_id=1, source_target_pairs={{0,112},{16,96},{32,80},{48,64},{64,48},{80,32},{96,16},{112,0}} | collective-permute-start | bytes 196616 | tf_op jit(solution)/shard_map/ppermute | solution.py:706
  137.2 7.1 %collective-permute-start.14 = (f32[2,4,2,8,128]{4,3,2,1,0:T(8,128)S(1)}, f32[2,4,2,8,128]{4,3,2,1,0:T(8,128)S(1)}, u32[]{:S(2)}, u32[]{:S(2)}) collective-permute-start(f32[2,4,2,8,128]{4,3,2,1,0:T(8,128)S(1)} %get-tuple-element.118), channel_id=1, source_target_pairs={{0,48},{1,49},{2,50},{3,51},{4,52},{5,53},{6,54},{7,55},{8,56},{9,... | collective-permute-start | bytes 196616 | tf_op jit(solution)/shard_map/ppermute | solution.py:641
  147.7 7.2 %collective-permute-start.15 = (f32[4,4,2,8,128]{4,3,2,1,0:T(8,128)S(1)}, f32[4,4,2,8,128]{4,3,2,1,0:T(8,128)S(1)}, u32[]{:S(2)}, u32[]{:S(2)}) collective-permute-start(f32[4,4,2,8,128]{4,3,2,1,0:T(8,128)S(1)} %pad_maximum_fusion.4), channel_id=1, source_target_pairs={{0,64},{1,65},{2,66},{3,67},{4,68},{5,69},{6,70},{7,71},{8,72},{9,... | collective-permute-start | bytes 393224 | tf_op jit(solution)/shard_map/ppermute | solution.py:641
  162.4 16.7 %all-to-all-start.2 = ((f32[16,128,128]{2,1,0:T(8,128)}), f32[16,128,128]{2,1,0:T(8,128)S(1)}, u32[]{:S(2)}, u32[]{:S(2)}) async-start(f32[16,128,128]{2,1,0:T(8,128)} %get-tuple-element.83), calls=%async_computation.2 | async-start | bytes 2097152 | tf_op jit(solution)/shard_map/all_to_all | solution.py:629
  179.2 38.8 %all-to-all-start.3 = ((f32[16,128,128]{2,1,0:T(8,128)}), f32[16,128,128]{2,1,0:T(8,128)S(1)}, u32[]{:S(2)}, u32[]{:S(2)}) async-start(f32[16,128,128]{2,1,0:T(8,128)} %get-tuple-element.85), calls=%async_computation.3 | async-start | bytes 2097152 | tf_op jit(solution)/shard_map/all_to_all | solution.py:629
  184.8 19.6 %collective-permute-start.19 = (f32[2,2,256,128]{3,2,1,0:T(8,128)S(1)}, f32[2,2,256,128]{3,2,1,0:T(8,128)S(1)}, u32[]{:S(2)}, u32[]{:S(2)}) collective-permute-start(f32[2,2,256,128]{3,2,1,0:T(8,128)S(1)} %get-tuple-element.92), channel_id=1, source_target_pairs={{0,4},{1,5},{2,6},{3,7},{4,8},{5,9},{6,10},{7,11},{8,12},{9,13},{1... | collective-permute-start | bytes 1572872 | tf_op jit(solution)/shard_map/ppermute | solution.py:641
  184.9 25.8 %collective-permute-start.20 = (f32[2,2,256,128]{3,2,1,0:T(8,128)S(1)}, f32[2,2,256,128]{3,2,1,0:T(8,128)S(1)}, u32[]{:S(2)}, u32[]{:S(2)}) collective-permute-start(f32[2,2,256,128]{3,2,1,0:T(8,128)S(1)} %get-tuple-element.93), channel_id=1, source_target_pairs={{0,8},{1,9},{2,10},{3,11},{4,12},{5,13},{6,14},{7,15},{8,0},{9,1},... | collective-permute-start | bytes 1572872 | tf_op jit(solution)/shard_map/ppermute | solution.py:641
  189.8 20.8 %collective-permute-start.21 = (f32[2,2,256,128]{3,2,1,0:T(8,128)S(1)}, f32[2,2,256,128]{3,2,1,0:T(8,128)S(1)}, u32[]{:S(2)}, u32[]{:S(2)}) collective-permute-start(f32[2,2,256,128]{3,2,1,0:T(8,128)S(1)} %get-tuple-element.94), channel_id=1, source_target_pairs={{0,12},{1,13},{2,14},{3,15},{4,0},{5,1},{6,2},{7,3},{8,4},{9,5},{1... | collective-permute-start | bytes 1572872 | tf_op jit(solution)/shard_map/ppermute | solution.py:641
  211.8 11.8 %collective-permute-start.22 = (f32[4,2,256,128]{3,2,1,0:T(8,128)}, f32[4,2,256,128]{3,2,1,0:T(8,128)}, u32[]{:S(2)}, u32[]{:S(2)}) collective-permute-start(f32[4,2,256,128]{3,2,1,0:T(8,128)} %pad_maximum_fusion.1), channel_id=1, source_target_pairs={{0,1},{1,0},{2,3},{3,2},{4,5},{5,4},{6,7},{7,6},{8,9},{9,8},{10,11... | collective-permute-start | bytes 3145736 | tf_op jit(solution)/shard_map/ppermute | solution.py:641
  219.9 26.1 %collective-permute-start.16 = (f32[2,2,256,128]{3,2,1,0:T(8,128)S(1)}, f32[2,2,256,128]{3,2,1,0:T(8,128)S(1)}, u32[]{:S(2)}, u32[]{:S(2)}) collective-permute-start(f32[2,2,256,128]{3,2,1,0:T(8,128)S(1)} %get-tuple-element.87), channel_id=1, source_target_pairs={{0,4},{1,5},{2,6},{3,7},{4,8},{5,9},{6,10},{7,11},{8,12},{9,13},{1... | collective-permute-start | bytes 1572872 | tf_op jit(solution)/shard_map/ppermute | solution.py:641
  220.0 26.0 %collective-permute-start.17 = (f32[2,2,256,128]{3,2,1,0:T(8,128)S(1)}, f32[2,2,256,128]{3,2,1,0:T(8,128)S(1)}, u32[]{:S(2)}, u32[]{:S(2)}) collective-permute-start(f32[2,2,256,128]{3,2,1,0:T(8,128)S(1)} %get-tuple-element.88), channel_id=1, source_target_pairs={{0,8},{1,9},{2,10},{3,11},{4,12},{5,13},{6,14},{7,15},{8,0},{9,1},... | collective-permute-start | bytes 1572872 | tf_op jit(solution)/shard_map/ppermute | solution.py:641
  220.4 25.8 %collective-permute-start.18 = (f32[2,2,256,128]{3,2,1,0:T(8,128)S(1)}, f32[2,2,256,128]{3,2,1,0:T(8,128)S(1)}, u32[]{:S(2)}, u32[]{:S(2)}) collective-permute-start(f32[2,2,256,128]{3,2,1,0:T(8,128)S(1)} %get-tuple-element.89), channel_id=1, source_target_pairs={{0,12},{1,13},{2,14},{3,15},{4,0},{5,1},{6,2},{7,3},{8,4},{9,5},{1... | collective-permute-start | bytes 1572872 | tf_op jit(solution)/shard_map/ppermute | solution.py:641
  (22 other events, 158.5 us)
where the time goes:
time: 255 us; the launch traced here: 253 us
  waiting for transfers between devices  92.1 us (36%)
  starting transfers between devices  63.7 us (25%)
  Pallas kernels  42 us (16%)
  local copies, waits for them, and re-layouts  38.8 us (15%)
  other arithmetic  15.5 us (6%)
    all_to_all x4, waiting for transfers between devices, exchange(): return lax.all_to_all(values, axes, split_axis=0, concat_axis=0, tiled=True)  48.1 us
    ppermute x22, waiting for transfers between devices, shifted(): lax.ppermute(values, AXES, offset_pairs(offset))  44.1 us
    ppermute x22, starting transfers between devices, shifted(): lax.ppermute(values, AXES, offset_pairs(offset))  38.8 us
    all_to_all x4, starting transfers between devices, exchange(): return lax.all_to_all(values, axes, split_axis=0, concat_axis=0, tiled=True)  23.5 us
    reshape x1, local copies, waits for them, and re-layouts, per_device(): packed = weight.reshape(2, C, 256, 128)  19.9 us
    convert_element_type x1, other arithmetic, weight_grad(): return (real * cotangent + imag * turned).astype(BF16)  12.5 us
    unnamed x36, local copies, waits for them, and re-layouts  7.87 us
    pallas_call x2, Pallas kernels, z_inverse_call(): pl.pallas_call(z_inverse_kernel, out_shape=struct(32, 16, 16, Z, kind=BF1...  7.72 us
  transfers between devices with their start and end apart: 28, of which 14 were waited for; matrix products, arithmetic and copies ran while one was open for 17% of the time, Pallas kernels for 11%

commit v1 on v0

--- a/solution.py
+++ b/solution.py
@@ -1,5 +1,6 @@
 import functools
 import math
+import typing
 
 import jax
 import jax.numpy as jnp
@@ -283,18 +284,16 @@
             columns.append(jnp.concatenate([received[s][target, rows] for s in range(4)], 0))
         values = table_dot(table[...], jnp.concatenate(columns, 1))
         for k in range(4):
-            out[target, k] = values[:, k * 128 : k * 128 + 128]
+            out[target % 2, target // 2, k] = values[:, k * 128 : k * 128 + 128]
 
 
 def sum_rows_kernel(place, *refs):
-    received, out = refs[:4], refs[4]
+    received, out = refs[:2], refs[2]
     for target in range(8):
         offset = (target % 4 + 4 - place[1]) % 4 * 2 + (target // 4 + 2 - place[0]) % 2
         for k in range(4):
             rows = slice(target * 16, target * 16 + 16)
-            total = (received[0][k, rows] + received[1][k, rows]) + (
-                received[2][k, rows] + received[3][k, rows]
-            )
+            total = received[0][k, rows] + received[1][k, rows]
             out[offset, k] = total.reshape(2, 8, 128)
 
 
@@ -419,17 +418,51 @@
     return jnp.stack([lax.axis_index("xh"), lax.axis_index("z")]).astype(jnp.int32)
 
 
-def call(kernel, out, grid, in_specs, out_specs, scratch=(), cost=None, grant=40):
-    return pl.pallas_call(
-        kernel,
+def call(
+    kernel, out, grid, in_specs, out_specs, scratch=(), cost=None, grant=40, place=None, aliases={}
+):
+    params = pltpu.CompilerParams(vmem_limit_bytes=grant * 2**20)
+    if place is None:
+        return pl.pallas_call(
+            kernel,
+            out_shape=out,
+            grid=grid,
+            in_specs=in_specs,
+            out_specs=out_specs,
+            scratch_shapes=list(scratch),
+            compiler_params=params,
+            cost_estimate=cost,
+        )
+
+    def fit(spec):
+        if isinstance(spec, Placed):
+            return pl.BlockSpec((None, spec.rows, spec.columns), lambda *a: (a[-1][0], 0, 0))
+        if spec.index_map is None:
+            return spec
+        return pl.BlockSpec(spec.block_shape, lambda *a: spec.index_map(*a[:-1]))
+
+    specs = [fit(spec) for spec in in_specs]
+    single = isinstance(out_specs, pl.BlockSpec)
+    built = pl.pallas_call(
+        lambda index, *refs: kernel(*refs),
         out_shape=out,
-        grid=grid,
-        in_specs=in_specs,
-        out_specs=out_specs,
-        scratch_shapes=list(scratch),
-        compiler_params=pltpu.CompilerParams(vmem_limit_bytes=grant * 2**20),
+        grid_spec=pltpu.PrefetchScalarGridSpec(
+            num_scalar_prefetch=1,
+            grid=grid or (1,),
+            in_specs=specs,
+            out_specs=fit(out_specs) if single else [fit(spec) for spec in out_specs],
+            scratch_shapes=list(scratch),
+        ),
+        input_output_aliases=aliases,
+        compiler_params=params,
         cost_estimate=cost,
     )
+    return lambda *operands: built(place, *operands)
+
+
+class Placed(typing.NamedTuple):
+    rows: int
+    columns: int
 
 
 def whole(*dims):
@@ -452,12 +485,13 @@
         [
             pl.BlockSpec((32, 4, 16, Z), lambda i: (0, i, 0, 0)),
             whole(256, 256),
-            whole(256, Z),
+            Placed(256, Z),
         ],
         [pl.BlockSpec((2, 1, 16, 2, 8, 128), lambda i: (0, i, 0, 0, 0, 0))] * 4,
         [pltpu.VMEM((16, 4, 32, Z), BF16)],
         estimate(3 * 2**30, 8 * 2**20),
         60,
+        own_place(),
     )(volume, jnp.asarray(swap_table()), table)
 
 
@@ -467,10 +501,11 @@
         struct(16, 16, 2, 8, 128),
         (4,),
         [pl.BlockSpec((1, 1, 256, 128), lambda i: (0, i, 0, 0))] * 4
-        + [pl.BlockSpec((4, 1, 256, 128), lambda i: (0, i, 0, 0)), whole(256, 256)],
+        + [pl.BlockSpec((4, 1, 256, 128), lambda i: (0, i, 0, 0)), Placed(256, 256)],
         pl.BlockSpec((16, 4, 2, 8, 128), lambda i: (0, i, 0, 0, 0)),
         (),
         estimate(2 * 2**30, 6 * 2**20),
+        place=own_place(),
     )(*[block.reshape(block.shape[:-4] + (256, 128)) for block in received], table)
 
 
@@ -481,12 +516,13 @@
         (4,),
         [
             pl.BlockSpec((32, 4, 16, Z), lambda i: (0, i, 0, 0)),
-            whole(256, Z),
+            Placed(256, Z),
         ],
         pl.BlockSpec((8, 4, 4, 2, 8, 128), lambda i: (0, 0, i, 0, 0, 0)),
         (),
         estimate(2 * 2**30, 8 * 2**20),
         60,
+        own_place(),
     )(volume, table)
 
 
@@ -508,12 +544,13 @@
 def y_forward_rows_call(received, table):
     return call(
         y_forward_rows_kernel,
-        struct(4, 4, 128, 128),
-        (),
-        [whole(4, 128, 128)] * 4 + [whole(256, 128)],
-        whole(4, 4, 128, 128),
+        struct(2, 2, 4, 128, 128),
+        (),
+        [whole(4, 128, 128)] * 4 + [Placed(256, 128)],
+        whole(2, 2, 4, 128, 128),
         (),
         estimate(2**20, 2**16),
+        place=own_place(),
     )(*received, table)
 
 
@@ -522,7 +559,7 @@
         sum_rows_kernel,
         struct(8, 4, 2, 8, 128),
         (),
-        [SCALARS] + [whole(4, 128, 128)] * 4,
+        [SCALARS] + [whole(4, 128, 128)] * 2,
         whole(8, 4, 2, 8, 128),
         (),
         estimate(2**20, 2**16),
@@ -595,28 +632,29 @@
         (2,),
         [
             pl.BlockSpec((16, 4, 2, 8, 128), lambda i: (0, i, 0, 0, 0)),
-            whole(512, 128),
+            Placed(512, 128),
         ],
         [pl.BlockSpec((2, 1, 256, 128), lambda i: (0, i, 0, 0))] * 4,
         (),
         estimate(2**30, 3 * 2**20),
+        place=own_place(),
     )(received.reshape(16, 8, 2, 8, 128), table)
 
 
 def z_inverse_call(received, table, half, others):
-    return pl.pallas_call(
+    return call(
         z_inverse_kernel,
-        out_shape=struct(32, 16, 16, Z, kind=BF16),
-        grid=(2,),
-        in_specs=[pl.BlockSpec((1, 1, 16, 2, 8, 128), lambda i: (0, i, 0, 0, 0, 0))] * 4
+        struct(32, 16, 16, Z, kind=BF16),
+        (2,),
+        [pl.BlockSpec((1, 1, 16, 2, 8, 128), lambda i: (0, i, 0, 0, 0, 0))] * 4
         + [pl.BlockSpec((4, 1, 16, 2, 8, 128), lambda i: (0, i, 0, 0, 0, 0))]
-        + [whole(256, 256), whole(256, Z)]
+        + [whole(256, 256), Placed(256, Z)]
         + [pl.BlockSpec(memory_space=pl.ANY)] * len(others),
-        out_specs=pl.BlockSpec((32, 4, 16, Z), lambda i: (0, i + 2 * half, 0, 0)),
-        scratch_shapes=[pltpu.VMEM((16, 4, 32, Z), BF16)],
-        input_output_aliases={7: 0} if others else {},
-        compiler_params=pltpu.CompilerParams(vmem_limit_bytes=40 * 2**20),
-        cost_estimate=estimate(3 * 2**29, 4 * 2**20),
+        pl.BlockSpec((32, 4, 16, Z), lambda i: (0, i + 2 * half, 0, 0)),
+        [pltpu.VMEM((16, 4, 32, Z), BF16)],
+        estimate(3 * 2**29, 4 * 2**20),
+        place=own_place(),
+        aliases={8: 0} if others else {},
     )(
         *[block.reshape(block.shape[:-2] + (16, 2, 8, 128)) for block in received],
         jnp.asarray(swap_table()),
@@ -646,13 +684,14 @@
 
 
 def by_place(build):
-    tables = np.stack(
-        [build(y, core, xl) for y in range(4) for core in range(2) for xl in range(2)]
+    return jnp.asarray(
+        np.stack([build(y, core, xl) for y in range(4) for core in range(2) for xl in range(2)])
     )
+
+
+def own_place():
     y, core, xl = (lax.axis_index(a) for a in ("y", "core", "xl"))
-    return lax.dynamic_index_in_dim(
-        jnp.asarray(tables), (y * 2 + core) * 2 + xl, 0, keepdims=False
-    )
+    return ((y * 2 + core) * 2 + xl).astype(jnp.int32).reshape(1)
 
 
 def first_order(y, core, sign):
@@ -733,16 +772,17 @@
     lines, blocks = barrier((lines, blocks))
     blocks = [shifted(blocks[i], y=i) for i in range(4)]
     planes = y_forward_call(cross(lines), by_place(y_columns_by_offset))
-    planes, blocks = barrier((planes, blocks))
     planes = exchange(planes, SECOND)
     blocks = y_forward_rows_call(blocks, by_place(y_columns_by_col))
-    blocks = [shifted(blocks[2 * i + j], xl=i, core=j) for i in range(2) for j in range(2)]
+    blocks = blocks[0] + shifted(blocks[1], core=1)
+    blocks = [blocks[0], shifted(blocks[1], xl=1)]
     spectra = x_forward_call(planes)
     mixed = mix_call(packed, spectra)
     mixed, blocks = barrier((mixed, blocks))
-    arrived = sum_rows_call(blocks)
-    arrived = [shifted(arrived[2 * i : 2 * i + 2], z=i) for i in range(4)]
-    partner, arrived = barrier((mirrored(mixed), arrived))
+    mixed, sums = barrier((mixed, sum_rows_call(blocks)))
+    arrived = [shifted(sums[2 * i : 2 * i + 2], z=i) for i in range(4)]
+    partner = mirrored(mixed)
+    partner, arrived = barrier((partner, arrived))
     crossed = shifted(jnp.stack([block[1] for block in arrived]), xh=1)
     back, cotangent = back_call(packed, mixed, partner, arrived + [crossed])
     y_table, z_table_here = by_place(y_rows_by_offset), by_place(z_rows_by_source)
@@ -751,6 +791,7 @@
     first = y_inverse_call(first, y_table)
     first = [shifted(block, y=i) for i, block in enumerate(first)]
     second = y_inverse_call(exchange(second, SECOND), y_table)
+    first, second = barrier((first, second))
     second = [shifted(block, y=i) for i, block in enumerate(second)]
     grad = weight_grad(spectra, cotangent)
     first, grad = barrier((first, grad))

time: 255 us -> 244 us (0.957)
  waiting for transfers between devices: 92.1 us -> 79.9 us
    all_to_all x4, waiting for transfers between devices: 48.1 us -> 31.4 us  [exchange(): return lax.all_to_all(values, axes, split_axis=0, concat_axis=0, tiled=True)]
    squeeze x6 -> x2, local copies, waits for them, and re-layouts: 6.2 us -> 0.07 us  [the longest x1 0.04 us: per_device(): blocks = [blocks[0], shifted(blocks[1], xl=1)]]
    ppermute x22 -> x21, waiting for transfers between devices: 44.1 us -> 48.5 us  [shifted(): lax.ppermute(values, AXES, offset_pairs(offset))]
    slice x12, local copies, waits for them, and re-layouts: 0.29 us -> 4.41 us  [cross(): block[1]]
    pallas_call x8, Pallas kernels: 28 us -> 30.6 us  [call(): return lambda *operands: built(place, *operands)]
    unnamed x36 -> x28, local copies, waits for them, and re-layouts: 7.87 us -> 10.3 us
    ppermute x22 -> x21, starting transfers between devices: 38.8 us -> 37.6 us  [shifted(): lax.ppermute(values, AXES, offset_pairs(offset))]
  transfers between devices with their start and end apart: 28 -> 27, of which waited for: 14 -> 17; matrix products, arithmetic and copies ran while one was open for 17% -> 16% of each run, Pallas kernels for 11% -> 10%
where the time goes in v1:
time: 244 us; the launch traced here: 243 us
  waiting for transfers between devices  79.9 us (33%)
  starting transfers between devices  63.4 us (26%)
  Pallas kernels  44.5 us (18%)
  local copies, waits for them, and re-layouts  39.2 us (16%)
  other arithmetic  14.7 us (6%)
    ppermute x21, waiting for transfers between devices, shifted(): lax.ppermute(values, AXES, offset_pairs(offset))  48.5 us
    ppermute x21, starting transfers between devices, shifted(): lax.ppermute(values, AXES, offset_pairs(offset))  37.6 us
    all_to_all x4, waiting for transfers between devices, exchange(): return lax.all_to_all(values, axes, split_axis=0, concat_axis=0, tiled=True)  31.4 us
    pallas_call x8, Pallas kernels, call(): return lambda *operands: built(place, *operands)  30.6 us
    all_to_all x4, starting transfers between devices, exchange(): return lax.all_to_all(values, axes, split_axis=0, concat_axis=0, tiled=True)  24.5 us
    reshape x1, local copies, waits for them, and re-layouts, per_device(): packed = weight.reshape(2, C, 256, 128)  19.9 us
    convert_element_type x1, other arithmetic, weight_grad(): return (real * cotangent + imag * turned).astype(BF16)  12.6 us
    unnamed x28, local copies, waits for them, and re-layouts  10.3 us
  transfers between devices with their start and end apart: 27, of which 17 were waited for; matrix products, arithmetic and copies ran while one was open for 16% of the time, Pallas kernels for 10%

profile of v1, /device:TPU:1, one launch (start us, length us, event | category | flops | bytes accessed | tf_op | source)
XLA Modules:
  0.0 242.8 jit_solution(17251456337455528626)
XLA Ops:
  0.6 5.8 %shard_map.167 = f32[8,4,16,2,8,128]{5,4,3,2,1,0:T(8,128)} custom-call(s32[1]{0:T(128)} %bitcast.index, bf16[32,16,16,256]{3,2,1,0:T(8,128)(2,1)} %refs_0_.1, bf16[16,256,256]{2,1,0:T(8,128)(2,1)} %constant.45.clone.refs_1_), custom_call_target="tpu_custom_call" | custom-call | flops 2147483648 | bytes 8388608 | tf_op jit(solution)/shard_map/pallas_call | solution.py:460
  6.5 8.3 %all-to-all-start = ((f32[8,4,16,2,8,128]{5,4,3,2,1,0:T(8,128)}), f32[8,4,16,2,8,128]{5,4,3,2,1,0:T(8,128)}, u32[]{:S(2)}, u32[]{:S(2)}) async-start(f32[8,4,16,2,8,128]{5,4,3,2,1,0:T(8,128)} %shard_map.167), calls=%async_computation | async-start | bytes 8388608 | tf_op jit(solution)/shard_map/all_to_all | solution.py:667
  14.8 6.5 %shard_map.168 = (f32[2,4,16,2,8,128]{5,4,3,2,1,0:T(8,128)}, f32[2,4,16,2,8,128]{5,4,3,2,1,0:T(8,128)}, f32[2,4,16,2,8,128]{5,4,3,2,1,0:T(8,128)}, f32[2,4,16,2,8,128]{5,4,3,2,1,0:T(8,128)}) custom-call(s32[1]{0:T(128)} %bitcast.index, bf16[32,16,16,256]{3,2,1,0:T(8,128)(2,1)} %refs_0_.2, bf16[256,256]{1,0:T(8,128)(2,1)} %constant.47.clone.refs_1_.refs_5_, ...), custom_call_target="tpu_custom_call" | custom-call | flops 3221225472 | bytes 8388608 | tf_op jit(solution)/shard_map/pallas_call | solution.py:460
  26.3 19.9 %reshape.97.weight.refs_1_ = bf16[2,32,256,128]{3,2,1,0:T(8,128)(2,1)} reshape(bf16[2,32,32,8,4,32]{5,4,3,2,1,0:T(4,128)(2,1)} %param.18) | data formatting | bytes 8388608 | tf_op jit(solution)/shard_map/reshape | solution.py:763
  46.2 17.3 %all-to-all-done = f32[8,4,16,2,8,128]{5,4,3,2,1,0:T(8,128)} async-done(((f32[8,4,16,2,8,128]{5,4,3,2,1,0:T(8,128)}), f32[8,4,16,2,8,128]{5,4,3,2,1,0:T(8,128)}, u32[]{:S(2)}, u32[]{:S(2)}) %all-to-all-start) | async-done | bytes 4194336 | tf_op jit(solution)/shard_map/all_to_all | solution.py:667
  63.5 4.9 %shard_map.169 = f32[2,4,2,4,2,16,128]{6,5,4,3,2,1,0:T(8,128)S(1)} custom-call(f32[8,4,256,128]{3,2,1,0:T(8,128)} %bitcast.3.received, bf16[128,256]{1,0:T(8,128)(2,1)S(1)} %copy-done.8), custom_call_target="tpu_custom_call" | custom-call | flops 1048576 | bytes 65536 | tf_op jit(solution)/shard_map/pallas_call | solution.py:530
  74.8 3.8 %collective-permute-done.3 = f32[4,4,16,2,8,128]{5,4,3,2,1,0:T(8,128)S(1)} collective-permute-done((f32[4,4,16,2,8,128]{5,4,3,2,1,0:T(8,128)S(1)}, f32[4,4,16,2,8,128]{5,4,3,2,1,0:T(8,128)S(1)}, u32[]{:S(2)}, u32[]{:S(2)}) %collective-permute-start.3) | collective-permute-done | bytes 2097184 | tf_op jit(solution)/shard_map/ppermute | solution.py:679
  78.6 4.5 %shard_map.170 = f32[16,16,2,8,128]{4,3,2,1,0:T(8,128)S(1)} custom-call(s32[1]{0:T(128)} %bitcast.index, f32[2,4,256,128]{3,2,1,0:T(8,128)S(1)} %bitcast.53, f32[2,4,256,128]{3,2,1,0:T(8,128)S(1)} %bitcast.54, f32[2,4,256,128]{3,2,1,0:T(8,128)} %bitcast.7.refs_2_, f32[2,4,256,128]{3,2,1,0:T(8,128)} %bitcast.8.refs_3_, f32[4,4,256,128]{3,2,1,0:T(8,128)S(1)} %bitcast.55, ...), custom_call_target="tpu_custom_call" | custom-call | flops 2147483648 | bytes 6291456 | tf_op jit(solution)/shard_map/pallas_call | solution.py:460
  84.4 6.8 %all-to-all-start.1 = ((f32[16,16,2,8,128]{4,3,2,1,0:T(8,128)}), f32[16,16,2,8,128]{4,3,2,1,0:T(8,128)S(1)}, u32[]{:S(2)}, u32[]{:S(2)}) async-start(f32[16,16,2,8,128]{4,3,2,1,0:T(8,128)} %copy-done.3), calls=%async_computation.1 | async-start | bytes 4194304 | tf_op jit(solution)/shard_map/all_to_all | solution.py:667
  94.5 4.1 %collective-permute-done.6.refs_3_ = f32[4,128,128]{2,1,0:T(8,128)S(1)} collective-permute-done((f32[4,128,128]{2,1,0:T(8,128)S(1)}, f32[4,128,128]{2,1,0:T(8,128)S(1)}, u32[]{:S(2)}, u32[]{:S(2)}) %collective-permute-start.6) | collective-permute-done | bytes 262176 | tf_op jit(solution)/shard_map/ppermute | solution.py:679
  98.5 3.1 %collective-permute-done.5.refs_2_ = f32[4,128,128]{2,1,0:T(8,128)S(1)} collective-permute-done((f32[4,128,128]{2,1,0:T(8,128)S(1)}, f32[4,128,128]{2,1,0:T(8,128)S(1)}, u32[]{:S(2)}, u32[]{:S(2)}) %collective-permute-start.5) | collective-permute-done | bytes 262176 | tf_op jit(solution)/shard_map/ppermute | solution.py:679
  101.6 6.9 %collective-permute-done.4.refs_1_ = f32[4,128,128]{2,1,0:T(8,128)S(1)} collective-permute-done((f32[4,128,128]{2,1,0:T(8,128)S(1)}, f32[4,128,128]{2,1,0:T(8,128)S(1)}, u32[]{:S(2)}, u32[]{:S(2)}) %collective-permute-start.4) | collective-permute-done | bytes 262176 | tf_op jit(solution)/shard_map/ppermute | solution.py:679
  114.1 7.4 %all-to-all-done.1 = f32[16,16,2,8,128]{4,3,2,1,0:T(8,128)S(1)} async-done(((f32[16,16,2,8,128]{4,3,2,1,0:T(8,128)}), f32[16,16,2,8,128]{4,3,2,1,0:T(8,128)S(1)}, u32[]{:S(2)}, u32[]{:S(2)}) %all-to-all-start.1) | async-done | bytes 2097184 | tf_op jit(solution)/shard_map/all_to_all | solution.py:667
  135.3 3.4 %collective-permute-start.14 = (f32[4,4,2,8,128]{4,3,2,1,0:T(8,128)S(1)}, f32[4,4,2,8,128]{4,3,2,1,0:T(8,128)S(1)}, u32[]{:S(2)}, u32[]{:S(2)}) collective-permute-start(f32[4,4,2,8,128]{4,3,2,1,0:T(8,128)S(1)} %pad_maximum_fusion.4), channel_id=1, source_target_pairs={{0,64},{1,65},{2,66},{3,67},{4,68},{5,69},{6,70},{7,71},{8,72},{9,... | collective-permute-start | bytes 393224 | tf_op jit(solution)/shard_map/ppermute | solution.py:679
  138.7 4.0 %collective-permute-done.14.refs_8_ = f32[4,4,2,8,128]{4,3,2,1,0:T(8,128)S(1)} collective-permute-done((f32[4,4,2,8,128]{4,3,2,1,0:T(8,128)S(1)}, f32[4,4,2,8,128]{4,3,2,1,0:T(8,128)S(1)}, u32[]{:S(2)}, u32[]{:S(2)}) %collective-permute-start.14) | collective-permute-done | bytes 131104 | tf_op jit(solution)/shard_map/ppermute | solution.py:679
  150.3 5.0 %all-to-all-start.2 = ((f32[16,128,128]{2,1,0:T(8,128)}), f32[16,128,128]{2,1,0:T(8,128)S(1)}, u32[]{:S(2)}, u32[]{:S(2)}) async-start(f32[16,128,128]{2,1,0:T(8,128)} %get-tuple-element.81), calls=%async_computation.2 | async-start | bytes 2097152 | tf_op jit(solution)/shard_map/all_to_all | solution.py:667
  160.8 6.7 %all-to-all-done.2 = f32[16,128,128]{2,1,0:T(8,128)S(1)} async-done(((f32[16,128,128]{2,1,0:T(8,128)}), f32[16,128,128]{2,1,0:T(8,128)S(1)}, u32[]{:S(2)}, u32[]{:S(2)}) %all-to-all-start.2) | async-done | bytes 1048608 | tf_op jit(solution)/shard_map/all_to_all | solution.py:667
  167.5 4.4 %all-to-all-start.3 = ((f32[16,128,128]{2,1,0:T(8,128)}), f32[16,128,128]{2,1,0:T(8,128)}, u32[]{:S(2)}, u32[]{:S(2)}) async-start(f32[16,128,128]{2,1,0:T(8,128)} %get-tuple-element.88), calls=%async_computation.3 | async-start | bytes 2097152 | tf_op jit(solution)/shard_map/all_to_all | solution.py:667
  180.3 12.6 %add_convert_fusion = bf16[2,32,32,8,4,32]{5,4,3,2,1,0:T(4,128)(2,1)} fusion(f32[2,32,8,4,32]{4,3,2,1,0:T(4,128)S(1)} %copy-done.12, f32[32,8,4,32]{3,2,1,0:T(4,128)} %mul.71, f32[2,32,8,4,32]{4,3,2,1,0:T(4,128)} %mul.68, f32[32,8,4,32]{3,2,1,0:T(4,128)} %mul.32), kind=kLoop, calls=%fused_computation | loop fusion | flops 8388608 | bytes 4980736 | tf_op jit(solution)/shard_map/convert_element_type | solution.py:758
  199.6 9.8 %collective-permute-start.21 = (f32[4,2,256,128]{3,2,1,0:T(8,128)S(1)}, f32[4,2,256,128]{3,2,1,0:T(8,128)S(1)}, u32[]{:S(2)}, u32[]{:S(2)}) collective-permute-start(f32[4,2,256,128]{3,2,1,0:T(8,128)S(1)} %pad_maximum_fusion.1), channel_id=1, source_target_pairs={{0,1},{1,0},{2,3},{3,2},{4,5},{5,4},{6,7},{7,6},{8,9},{9,8},{10,11... | collective-permute-start | bytes 3145736 | tf_op jit(solution)/shard_map/ppermute | solution.py:679
  214.1 4.3 %shard_map.179.refs_7_ = bf16[32,16,16,256]{3,2,1,0:T(8,128)(2,1)} custom-call(s32[1]{0:T(128)} %bitcast.index, f32[2,2,16,2,8,128]{5,4,3,2,1,0:T(8,128)S(1)} %bitcast.58, f32[2,2,16,2,8,128]{5,4,3,2,1,0:T(8,128)S(1)} %bitcast.59, f32[2,2,16,2,8,128]{5,4,3,2,1,0:T(8,128)} %bitcast.26.refs_2_, f32[2,2,16,2,8,128]{5,4,3,2,1,0:T(8,128)} %bitcast.27.refs_3_, ...), custom_call_target="tpu_custom_call" | custom-call | flops 1610612736 | bytes 4194304 | tf_op jit(solution)/shard_map/pallas_call | solution.py:460
  218.4 5.7 %collective-permute-done.18 = f32[2,2,256,128]{3,2,1,0:T(8,128)S(1)} collective-permute-done((f32[2,2,256,128]{3,2,1,0:T(8,128)S(1)}, f32[2,2,256,128]{3,2,1,0:T(8,128)S(1)}, u32[]{:S(2)}, u32[]{:S(2)}) %collective-permute-start.18) | collective-permute-done | bytes 524320 | tf_op jit(solution)/shard_map/ppermute | solution.py:679
  224.1 11.4 %collective-permute-done.19 = f32[2,2,256,128]{3,2,1,0:T(8,128)S(1)} collective-permute-done((f32[2,2,256,128]{3,2,1,0:T(8,128)S(1)}, f32[2,2,256,128]{3,2,1,0:T(8,128)S(1)}, u32[]{:S(2)}, u32[]{:S(2)}) %collective-permute-start.19) | collective-permute-done | bytes 524320 | tf_op jit(solution)/shard_map/ppermute | solution.py:679
  239.4 3.4 %shard_map.180 = bf16[32,16,16,256]{3,2,1,0:T(8,128)(2,1)} custom-call(s32[1]{0:T(128)} %bitcast.index, f32[2,2,16,2,8,128]{5,4,3,2,1,0:T(8,128)S(1)} %bitcast.60, f32[2,2,16,2,8,128]{5,4,3,2,1,0:T(8,128)S(1)} %bitcast.61, f32[2,2,16,2,8,128]{5,4,3,2,1,0:T(8,128)S(1)} %bitcast.62, ...), custom_call_target="tpu_custom_call", output_to_operand_aliasing={{}: (8, {})} | custom-call | flops 1610612736 | bytes 4194304 | tf_op jit(solution)/shard_map/pallas_call | solution.py:460
  (115 shorter events, 71.7 us)
Async XLA Ops:
  6.5 57.0 %all-to-all-start = ((f32[8,4,16,2,8,128]{5,4,3,2,1,0:T(8,128)}), f32[8,4,16,2,8,128]{5,4,3,2,1,0:T(8,128)}, u32[]{:S(2)}, u32[]{:S(2)}) async-start(f32[8,4,16,2,8,128]{5,4,3,2,1,0:T(8,128)} %shard_map.167), calls=%async_computation | async-start | bytes 8388608 | tf_op jit(solution)/shard_map/all_to_all | solution.py:667
  21.3 47.1 %collective-permute-start = (f32[2,4,16,2,8,128]{5,4,3,2,1,0:T(8,128)}, f32[2,4,16,2,8,128]{5,4,3,2,1,0:T(8,128)S(1)}, u32[]{:S(2)}, u32[]{:S(2)}) collective-permute-start(f32[2,4,16,2,8,128]{5,4,3,2,1,0:T(8,128)} %get-tuple-element.61), channel_id=1, source_target_pairs={{0,4},{1,5},{2,6},{3,7},{4,8},{5,9},{6,10},{7,11},{8,12},{9,13},{1... | collective-permute-start | bytes 3145736 | tf_op jit(solution)/shard_map/ppermute | solution.py:679
  22.6 47.6 %collective-permute-start.1 = (f32[2,4,16,2,8,128]{5,4,3,2,1,0:T(8,128)}, f32[2,4,16,2,8,128]{5,4,3,2,1,0:T(8,128)}, u32[]{:S(2)}, u32[]{:S(2)}) collective-permute-start(f32[2,4,16,2,8,128]{5,4,3,2,1,0:T(8,128)} %get-tuple-element.62), channel_id=1, source_target_pairs={{0,8},{1,9},{2,10},{3,11},{4,12},{5,13},{6,14},{7,15},{8,0},{9,1},... | collective-permute-start | bytes 3145736 | tf_op jit(solution)/shard_map/ppermute | solution.py:679
  25.2 45.0 %collective-permute-start.2 = (f32[2,4,16,2,8,128]{5,4,3,2,1,0:T(8,128)}, f32[2,4,16,2,8,128]{5,4,3,2,1,0:T(8,128)}, u32[]{:S(2)}, u32[]{:S(2)}) collective-permute-start(f32[2,4,16,2,8,128]{5,4,3,2,1,0:T(8,128)} %get-tuple-element.63), channel_id=1, source_target_pairs={{0,12},{1,13},{2,14},{3,15},{4,0},{5,1},{6,2},{7,3},{8,4},{9,5},{1... | collective-permute-start | bytes 3145736 | tf_op jit(solution)/shard_map/ppermute | solution.py:679
  72.8 5.8 %collective-permute-start.3 = (f32[4,4,16,2,8,128]{5,4,3,2,1,0:T(8,128)S(1)}, f32[4,4,16,2,8,128]{5,4,3,2,1,0:T(8,128)S(1)}, u32[]{:S(2)}, u32[]{:S(2)}) collective-permute-start(f32[4,4,16,2,8,128]{5,4,3,2,1,0:T(8,128)S(1)} %pad_maximum_fusion), channel_id=1, source_target_pairs={{0,1},{1,0},{2,3},{3,2},{4,5},{5,4},{6,7},{7,6},{8,9},{9,8},{10,11... | collective-permute-start | bytes 6291464 | tf_op jit(solution)/shard_map/ppermute | solution.py:679
  84.4 37.1 %all-to-all-start.1 = ((f32[16,16,2,8,128]{4,3,2,1,0:T(8,128)}), f32[16,16,2,8,128]{4,3,2,1,0:T(8,128)S(1)}, u32[]{:S(2)}, u32[]{:S(2)}) async-start(f32[16,16,2,8,128]{4,3,2,1,0:T(8,128)} %copy-done.3), calls=%async_computation.1 | async-start | bytes 4194304 | tf_op jit(solution)/shard_map/all_to_all | solution.py:667
  91.3 7.3 %collective-permute-start.6 = (f32[4,128,128]{2,1,0:T(8,128)S(1)}, f32[4,128,128]{2,1,0:T(8,128)S(1)}, u32[]{:S(2)}, u32[]{:S(2)}) collective-permute-start(f32[4,128,128]{2,1,0:T(8,128)S(1)} %get-tuple-element.112), channel_id=1, source_target_pairs={{0,12},{1,13},{2,14},{3,15},{4,0},{5,1},{6,2},{7,3},{8,4},{9,5},{1... | collective-permute-start | bytes 786440 | tf_op jit(solution)/shard_map/ppermute | solution.py:679
  93.2 8.4 %collective-permute-start.5 = (f32[4,128,128]{2,1,0:T(8,128)S(1)}, f32[4,128,128]{2,1,0:T(8,128)S(1)}, u32[]{:S(2)}, u32[]{:S(2)}) collective-permute-start(f32[4,128,128]{2,1,0:T(8,128)S(1)} %get-tuple-element.113), channel_id=1, source_target_pairs={{0,8},{1,9},{2,10},{3,11},{4,12},{5,13},{6,14},{7,15},{8,0},{9,1},... | collective-permute-start | bytes 786440 | tf_op jit(solution)/shard_map/ppermute | solution.py:679
  94.1 14.5 %collective-permute-start.4 = (f32[4,128,128]{2,1,0:T(8,128)S(1)}, f32[4,128,128]{2,1,0:T(8,128)S(1)}, u32[]{:S(2)}, u32[]{:S(2)}) collective-permute-start(f32[4,128,128]{2,1,0:T(8,128)S(1)} %get-tuple-element.114), channel_id=1, source_target_pairs={{0,4},{1,5},{2,6},{3,7},{4,8},{5,9},{6,10},{7,11},{8,12},{9,13},{1... | collective-permute-start | bytes 786440 | tf_op jit(solution)/shard_map/ppermute | solution.py:679
  112.6 14.2 %collective-permute-start.8 = (f32[4,128,128]{2,1,0:T(8,128)S(1)}, f32[4,128,128]{2,1,0:T(8,128)S(1)}, u32[]{:S(2)}, u32[]{:S(2)}) collective-permute-start(f32[4,128,128]{2,1,0:T(8,128)S(1)} %get-tuple-element.116), channel_id=1, source_target_pairs={{0,2},{1,3},{2,0},{3,1},{4,6},{5,7},{6,4},{7,5},{8,10},{9,11},{10,... | collective-permute-start | bytes 786440 | tf_op jit(solution)/shard_map/ppermute | solution.py:679
  127.4 3.6 %collective-permute-start.9 = (f32[2,32,1,32]{3,2,1,0:T(1,128)S(1)}, f32[2,32,1,32]{3,2,1,0:T(1,128)S(1)}, u32[]{:S(2)}, u32[]{:S(2)}) collective-permute-start(f32[2,32,1,32]{3,2,1,0:T(1,128)S(1)} %slice.143), channel_id=1, source_target_pairs={{16,112},{32,96},{48,80},{64,64},{80,48},{96,32},{112,16}} | collective-permute-start | bytes 24584 | tf_op jit(solution)/shard_map/ppermute | solution.py:746
  130.2 4.7 %collective-permute-start.12 = (f32[2,4,2,8,128]{4,3,2,1,0:T(8,128)S(1)}, f32[2,4,2,8,128]{4,3,2,1,0:T(8,128)S(1)}, u32[]{:S(2)}, u32[]{:S(2)}) collective-permute-start(f32[2,4,2,8,128]{4,3,2,1,0:T(8,128)S(1)} %get-tuple-element.123), channel_id=1, source_target_pairs={{0,32},{1,33},{2,34},{3,35},{4,36},{5,37},{6,38},{7,39},{8,40},{9,... | collective-permute-start | bytes 196616 | tf_op jit(solution)/shard_map/ppermute | solution.py:679
  130.2 5.0 %collective-permute-start.11 = (f32[2,4,2,8,128]{4,3,2,1,0:T(8,128)S(1)}, f32[2,4,2,8,128]{4,3,2,1,0:T(8,128)S(1)}, u32[]{:S(2)}, u32[]{:S(2)}) collective-permute-start(f32[2,4,2,8,128]{4,3,2,1,0:T(8,128)S(1)} %get-tuple-element.124), channel_id=1, source_target_pairs={{0,16},{1,17},{2,18},{3,19},{4,20},{5,21},{6,22},{7,23},{8,24},{9,... | collective-permute-start | bytes 196616 | tf_op jit(solution)/shard_map/ppermute | solution.py:679
  135.3 7.4 %collective-permute-start.14 = (f32[4,4,2,8,128]{4,3,2,1,0:T(8,128)S(1)}, f32[4,4,2,8,128]{4,3,2,1,0:T(8,128)S(1)}, u32[]{:S(2)}, u32[]{:S(2)}) collective-permute-start(f32[4,4,2,8,128]{4,3,2,1,0:T(8,128)S(1)} %pad_maximum_fusion.4), channel_id=1, source_target_pairs={{0,64},{1,65},{2,66},{3,67},{4,68},{5,69},{6,70},{7,71},{8,72},{9,... | collective-permute-start | bytes 393224 | tf_op jit(solution)/shard_map/ppermute | solution.py:679
  150.3 17.2 %all-to-all-start.2 = ((f32[16,128,128]{2,1,0:T(8,128)}), f32[16,128,128]{2,1,0:T(8,128)S(1)}, u32[]{:S(2)}, u32[]{:S(2)}) async-start(f32[16,128,128]{2,1,0:T(8,128)} %get-tuple-element.81), calls=%async_computation.2 | async-start | bytes 2097152 | tf_op jit(solution)/shard_map/all_to_all | solution.py:667
  167.5 25.4 %all-to-all-start.3 = ((f32[16,128,128]{2,1,0:T(8,128)}), f32[16,128,128]{2,1,0:T(8,128)}, u32[]{:S(2)}, u32[]{:S(2)}) async-start(f32[16,128,128]{2,1,0:T(8,128)} %get-tuple-element.88), calls=%async_computation.3 | async-start | bytes 2097152 | tf_op jit(solution)/shard_map/all_to_all | solution.py:667
  176.1 21.4 %collective-permute-start.15 = (f32[2,2,256,128]{3,2,1,0:T(8,128)}, f32[2,2,256,128]{3,2,1,0:T(8,128)S(1)}, u32[]{:S(2)}, u32[]{:S(2)}) collective-permute-start(f32[2,2,256,128]{3,2,1,0:T(8,128)} %get-tuple-element.85), channel_id=1, source_target_pairs={{0,4},{1,5},{2,6},{3,7},{4,8},{5,9},{6,10},{7,11},{8,12},{9,13},{1... | collective-permute-start | bytes 1572872 | tf_op jit(solution)/shard_map/ppermute | solution.py:679
  176.8 20.7 %collective-permute-start.16 = (f32[2,2,256,128]{3,2,1,0:T(8,128)}, f32[2,2,256,128]{3,2,1,0:T(8,128)}, u32[]{:S(2)}, u32[]{:S(2)}) collective-permute-start(f32[2,2,256,128]{3,2,1,0:T(8,128)} %get-tuple-element.86), channel_id=1, source_target_pairs={{0,8},{1,9},{2,10},{3,11},{4,12},{5,13},{6,14},{7,15},{8,0},{9,1},... | collective-permute-start | bytes 1572872 | tf_op jit(solution)/shard_map/ppermute | solution.py:679
  178.8 18.7 %collective-permute-start.17 = (f32[2,2,256,128]{3,2,1,0:T(8,128)}, f32[2,2,256,128]{3,2,1,0:T(8,128)}, u32[]{:S(2)}, u32[]{:S(2)}) collective-permute-start(f32[2,2,256,128]{3,2,1,0:T(8,128)} %get-tuple-element.87), channel_id=1, source_target_pairs={{0,12},{1,13},{2,14},{3,15},{4,0},{5,1},{6,2},{7,3},{8,4},{9,5},{1... | collective-permute-start | bytes 1572872 | tf_op jit(solution)/shard_map/ppermute | solution.py:679
  199.6 14.5 %collective-permute-start.21 = (f32[4,2,256,128]{3,2,1,0:T(8,128)S(1)}, f32[4,2,256,128]{3,2,1,0:T(8,128)S(1)}, u32[]{:S(2)}, u32[]{:S(2)}) collective-permute-start(f32[4,2,256,128]{3,2,1,0:T(8,128)S(1)} %pad_maximum_fusion.1), channel_id=1, source_target_pairs={{0,1},{1,0},{2,3},{3,2},{4,5},{5,4},{6,7},{7,6},{8,9},{9,8},{10,11... | collective-permute-start | bytes 3145736 | tf_op jit(solution)/shard_map/ppermute | solution.py:679
  209.4 14.7 %collective-permute-start.18 = (f32[2,2,256,128]{3,2,1,0:T(8,128)S(1)}, f32[2,2,256,128]{3,2,1,0:T(8,128)S(1)}, u32[]{:S(2)}, u32[]{:S(2)}) collective-permute-start(f32[2,2,256,128]{3,2,1,0:T(8,128)S(1)} %get-tuple-element.94), channel_id=1, source_target_pairs={{0,4},{1,5},{2,6},{3,7},{4,8},{5,9},{6,10},{7,11},{8,12},{9,13},{1... | collective-permute-start | bytes 1572872 | tf_op jit(solution)/shard_map/ppermute | solution.py:679
  210.0 25.5 %collective-permute-start.19 = (f32[2,2,256,128]{3,2,1,0:T(8,128)S(1)}, f32[2,2,256,128]{3,2,1,0:T(8,128)S(1)}, u32[]{:S(2)}, u32[]{:S(2)}) collective-permute-start(f32[2,2,256,128]{3,2,1,0:T(8,128)S(1)} %get-tuple-element.95), channel_id=1, source_target_pairs={{0,8},{1,9},{2,10},{3,11},{4,12},{5,13},{6,14},{7,15},{8,0},{9,1},... | collective-permute-start | bytes 1572872 | tf_op jit(solution)/shard_map/ppermute | solution.py:679
  212.1 23.6 %collective-permute-start.20 = (f32[2,2,256,128]{3,2,1,0:T(8,128)S(1)}, f32[2,2,256,128]{3,2,1,0:T(8,128)S(1)}, u32[]{:S(2)}, u32[]{:S(2)}) collective-permute-start(f32[2,2,256,128]{3,2,1,0:T(8,128)S(1)} %get-tuple-element.96), channel_id=1, source_target_pairs={{0,12},{1,13},{2,14},{3,15},{4,0},{5,1},{6,2},{7,3},{8,4},{9,5},{1... | collective-permute-start | bytes 1572872 | tf_op jit(solution)/shard_map/ppermute | solution.py:679
  235.8 3.5 %collective-permute-start.22 = (f32[4,2,256,128]{3,2,1,0:T(8,128)S(1)}, f32[4,2,256,128]{3,2,1,0:T(8,128)S(1)}, u32[]{:S(2)}, u32[]{:S(2)}) collective-permute-start(f32[4,2,256,128]{3,2,1,0:T(8,128)S(1)} %pad_maximum_fusion.2), channel_id=1, source_target_pairs={{0,1},{1,0},{2,3},{3,2},{4,5},{5,4},{6,7},{7,6},{8,9},{9,8},{10,11... | collective-permute-start | bytes 3145736 | tf_op jit(solution)/shard_map/ppermute | solution.py:679
  (17 other events, 162.0 us)
